TPU v7x, 32 devices: a whole 2x2x4 slice. The times are simulated.
32 devices in a mesh: dp: 16 (over z, x, core), blk: 2 (over y).
Axes of the slice: x: 2, y: 2, z: 4, core: 2. Of those that a mesh axis runs over, the one named last changes fastest.
Arguments:
- attn_cols: bfloat16 [4096, 7168], P('blk', 'dp'), may hold values from -6 to 6
- residual: bfloat16 [4096, 7168], P(('blk', 'dp')), may hold values from -80 to 80
- norm_gain: bfloat16 [7168], replicated, may hold values from 0.5 to 1.5
- router_weight: bfloat16 [7168, 16], replicated, may hold values from -0.0625 to 0.0625
- expert_ids: int32 [4096, 2], P(('blk', 'dp')), may hold values from 0 to 15, all different within a row; in each aligned block of 128 rows (0 to 127, 128 to 255, ...) at most 20 rows name the same one
- gate_weight: bfloat16 [16, 7168, 1024], P('dp', None, 'blk'), may hold values from -0.0625 to 0.0625
- up_weight: bfloat16 [16, 7168, 1024], P('dp', None, 'blk'), may hold values from -0.0625 to 0.0625
- down_weight: bfloat16 [16, 7168, 1024], P('dp', 'blk'), may hold values from -0.1875 to 0.1875
Outputs:
- layer_out: bfloat16 [4096, 7168], P(('blk', 'dp'))
Inputs may be any that keep to these rules, and one draw needn't show every extreme that they name: `expert_ids`: within each aligned block of 128 rows (the rows of one device) no expert is named by more than 20 rows, and in some block some expert is named by exactly 20 rows; the 2 experts of a row differ.
All inputs are finite; a program needn't handle non-finite values.
Results may differ from a plain program's by a relative error of at most 0.0044.
Values may be sent and summed in bfloat16 or wider, within the bound.
No kernel may reach another device: no remote copies, remote signals or barrier semaphores. Data moves between devices by JAX's collectives and lax.ppermute only.
A program may use at most 192 MiB of HBM per device.

v0:
```python
import jax
import jax.numpy as jnp
from jax import lax
from jax.sharding import PartitionSpec as P


def body(
    attn_cols, residual, norm_gain, router_weight, expert_ids, gate_weight, up_weight, down_weight
):
    regrouped = lax.all_to_all(attn_cols, "dp", split_axis=0, concat_axis=1, tiled=True)
    tok_rows = residual.shape[0]
    width = residual.shape[1]
    fanout = expert_ids.shape[1]
    experts = router_weight.shape[1]
    exp_local = gate_weight.shape[0]
    groups = lax.axis_size("dp")
    capacity = max(2, (5 * tok_rows * fanout + 4 * experts - 1) // (4 * experts))
    stream = residual.astype(jnp.float32) + regrouped.astype(jnp.float32)
    meansq = jnp.mean(stream * stream, axis=1, keepdims=True)
    normed = (stream * lax.rsqrt(meansq + 1e-06) * norm_gain.astype(jnp.float32)).astype(
        jnp.bfloat16
    )
    affinity = jax.nn.sigmoid(jnp.dot(normed, router_weight, preferred_element_type=jnp.float32))
    chosen = jnp.take_along_axis(affinity, expert_ids, axis=1)
    weights = 2.5 * chosen / jnp.sum(chosen, axis=1, keepdims=True)
    flat_ids = expert_ids.reshape(-1)
    onehot = (flat_ids[:, None] == jnp.arange(experts, dtype=jnp.int32)[None, :]).astype(jnp.int32)
    before = jnp.cumsum(onehot, axis=0) - onehot
    ranks = jnp.sum(before * onehot, axis=1)
    slots = flat_ids * capacity + ranks
    outgoing = jnp.zeros((experts * capacity, width), jnp.bfloat16)
    outgoing = outgoing.at[slots].set(jnp.repeat(normed, fanout, axis=0))
    arrived = lax.all_to_all(
        outgoing.reshape(groups, exp_local * capacity, width),
        "dp",
        split_axis=0,
        concat_axis=0,
        tiled=True,
    )
    arrived = arrived.reshape(groups, exp_local, capacity, width)

    def project_in(piece):
        return jnp.einsum("secd,edf->secf", arrived, piece, preferred_element_type=jnp.float32)

    gated = project_in(lax.all_gather(gate_weight, "blk", axis=2, tiled=True))
    upward = project_in(lax.all_gather(up_weight, "blk", axis=2, tiled=True))
    hidden = (jax.nn.silu(gated) * upward).astype(jnp.bfloat16)
    produced = jnp.einsum(
        "secf,edf->secd",
        hidden,
        lax.all_gather(down_weight, "blk", axis=1, tiled=True),
        preferred_element_type=jnp.float32,
    ).astype(jnp.bfloat16)
    results = produced.reshape(groups, exp_local * capacity, width)
    returned = lax.all_to_all(results, "dp", split_axis=0, concat_axis=0, tiled=True).reshape(
        experts * capacity, width
    )
    picked = returned[slots].reshape(tok_rows, fanout, width)
    summed = stream
    for member in range(fanout):
        summed = summed + weights[:, member : member + 1] * picked[:, member].astype(jnp.float32)
    return summed.astype(jnp.bfloat16)


def solution(mesh):
    return jax.shard_map(
        body,
        mesh=mesh,
        in_specs=(
            P("blk", "dp"),
            P(("blk", "dp"), None),
            P(),
            P(),
            P(("blk", "dp"), None),
            P("dp", None, "blk"),
            P("dp", None, "blk"),
            P("dp", "blk", None),
        ),
        out_specs=P(("blk", "dp"), None),
        check_vma=False,
    )
```

profile of v0, /device:TPU:11, one launch (start us, length us, event | category | flops | bytes accessed | tf_op | source)
XLA Modules:
  0.0 756.3 jit_solution(12824531397321000745)
XLA Ops:
  6.5 0.0 copy-start
  6.5 0.0 all-gather.4.cloned.1.call-start
  6.5 0.7 all-gather.4.cloned.1.call-update
  7.3 0.0 all-gather.6.cloned.1.call-start
  7.3 0.7 all-gather.6.cloned.1.call-update
  8.0 0.0 copy-done
  8.0 1.7 copy_bitcast_fusion
  9.7 6.6 all-to-all-start
  16.3 0.0 copy-start.5
  16.3 0.0 all-gather.8.cloned.1.call-start
  16.4 0.7 all-gather.8.cloned.1.call-update
  17.0 0.0 copy-done.5
  17.1 0.0 copy-start.6
  17.1 0.1 copy.61
  17.2 0.1 eq.29
  17.3 0.1 eq.25
  17.5 4.2 copy.56
  21.7 0.0 copy-done.6
  21.7 0.6 reduce-window.6
  22.3 0.2 slice_reduce_fusion
  22.5 0.1 copy.60
  22.6 0.1 mul.82
  22.8 0.1 fusion.28
  22.9 35.6 %all-to-all-done = bf16[16,128,448]{1,2,0:T(8,128)(2,1)S(1)} async-done(((bf16[16,128,448]{1,2,0:T(8,128)(2,1)}), bf16[16,128,448]{1,2,0:T(8,128)(2,1)S(1)}, u32[]{:S(2)}, u32[]{:S(2)}) %all-to-all-start) | async-done | bytes 1835040 | tf_op jit(solution)/shard_map/all_to_all | solution.py:10
  58.5 0.0 copy-start.2
  58.5 0.0 copy-start.3
  58.5 3.2 multiply_reduce_fusion
  61.7 0.0 copy-done.3
  61.7 3.9 multiply_convert_fusion
  65.6 0.0 copy-done.2
  65.6 3.9 copy.64
  69.5 5.0 broadcast_in_dim.18
  74.6 8.4 %reshape.139 = bf16[256,7168]{1,0:T(8,128)(2,1)} reshape(bf16[128,2,7168]{2,1,0:T(2,128)(2,1)} %broadcast_in_dim.18) | data formatting | bytes 7340032 | tf_op jit(solution)/shard_map/reshape | solution.py:32
  82.9 9.7 %scatter_custom_fusion = bf16[320,7168]{1,0:T(8,128)(2,1)} fusion(s32[256]{0:T(256)S(1)} %bitcast.104, bf16[256,7168]{1,0:T(8,128)(2,1)} %reshape.139, bf16[]{:T(256)} %constant.38.clone.1), kind=kCustom, calls=%fused_computation.18 | custom fusion | bytes 4588032 | tf_op jit(solution)/shard_map/scatter | solution.py:32
  92.6 7.2 reshape.111
  99.8 125.2 %all_to_all.23 = bf16[16,20,7168]{2,1,0:T(8,128)(2,1)} all-to-all(bf16[16,20,7168]{2,1,0:T(8,128)(2,1)} %reshape.111), channel_id=1, replica_groups=mesh['dp'=16,'blk'=2] {'dp'}, dimensions={0} | all-to-all | bytes 9175040 | tf_op jit(solution)/shard_map/all_to_all | solution.py:33
  225.1 0.0 all-gather.4.cloned.1.call-done
  225.1 10.8 %fusion.4 = f32[16,20,1024]{2,1,0:T(8,128)S(1)} fusion(bf16[16,20,7168]{2,1,0:T(8,128)(2,1)} %all_to_all.23, bf16[1,7168,1024]{2,1,0:T(8,128)(2,1)} %all-gather.4.cloned.1.call-done), kind=kOutput, calls=%fused_computation.7 | convolution fusion | flops 4697620480 | bytes 20578304 | tf_op jit(solution)/shard_map/secd,edf->secf/dot_general | solution.py:43
  235.9 126.9 %all-gather.6.cloned.1.call-done = bf16[1,7168,1024]{2,1,0:T(8,128)(2,1)} async-done(((bf16[1,7168,512]{2,1,0:T(8,128)(2,1)}), bf16[1,7168,1024]{2,1,0:T(8,128)(2,1)}) %all-gather.6.cloned.1.call-update) | async-done | bytes 14680080 | tf_op jit(solution)/shard_map/all_gather | solution.py:46
  362.7 10.8 %fusion.20 = bf16[16,20,1024]{2,1,0:T(8,128)(2,1)S(1)} fusion(bf16[16,20,7168]{2,1,0:T(8,128)(2,1)} %all_to_all.23, bf16[1,7168,1024]{2,1,0:T(8,128)(2,1)} %all-gather.6.cloned.1.call-done, f32[16,20,1024]{2,1,0:T(8,128)S(1)} %fusion.4), kind=kOutput, calls=%fused_computation.28 | convolution fusion | flops 4699586560 | bytes 21233664 | tf_op jit(solution)/shard_map/secd,edf->secf/dot_general | solution.py:43
  373.6 166.3 %all-gather.8.cloned.1.call-done = bf16[1,7168,1024]{2,1,0:T(8,128)(2,1)} async-done(((bf16[1,3584,1024]{2,1,0:T(8,128)(2,1)}), bf16[1,7168,1024]{2,1,0:T(8,128)(2,1)}) %all-gather.8.cloned.1.call-update) | async-done | bytes 14680080 | tf_op jit(solution)/shard_map/all_gather | solution.py:51
  539.9 21.2 %fusion.6 = bf16[16,20,7168]{2,1,0:T(8,128)(2,1)} fusion(bf16[16,20,1024]{2,1,0:T(8,128)(2,1)S(1)} %fusion.20, bf16[1,7168,1024]{2,1,0:T(8,128)(2,1)} %all-gather.8.cloned.1.call-done), kind=kOutput, calls=%fused_computation.9 | convolution fusion | flops 4699914240 | bytes 19922944 | tf_op jit(solution)/shard_map/secf,edf->secd/dot_general | solution.py:48
  561.1 0.0 copy-start.4
  561.1 6.5 all-to-all-start.2
  567.6 0.1 copy.58
  567.7 0.1 reshape.129
  567.9 0.0 copy-done.4
  567.9 1.9 fusion.25
  569.8 2.0 gather_fusion.1
  571.8 0.1 reshape.132
  571.9 0.1 copy.59
  572.0 116.1 %all-to-all-done.2 = bf16[16,20,7168]{2,1,0:T(8,128)(2,1)} async-done(((bf16[16,20,7168]{2,1,0:T(8,128)(2,1)}), bf16[16,20,7168]{2,1,0:T(8,128)(2,1)}, u32[]{:S(2)}, u32[]{:S(2)}) %all-to-all-start.2) | async-done | bytes 4587552 | tf_op jit(solution)/shard_map/all_to_all | solution.py:55
  688.2 7.4 reshape.116
  695.5 10.9 %gather_fusion = bf16[256,7168]{1,0:T(8,128)(2,1)} fusion(bf16[320,7168]{1,0:T(8,128)(2,1)} %reshape.116, s32[1024]{0:T(1024)S(1)} %pad_clamp_fusion), kind=kCustom, calls=%fused_computation | custom fusion | bytes 7341056 | tf_op jit(solution)/shard_map/gather | solution.py:58
  706.4 8.1 %reshape.117 = bf16[128,2,7168]{2,1,0:T(2,128)(2,1)} reshape(bf16[256,7168]{1,0:T(8,128)(2,1)} %gather_fusion) | data formatting | bytes 7340032 | tf_op jit(solution)/shard_map/reshape | solution.py:58
  714.5 8.9 %fusion.31 = (bf16[128,1,7168]{2,1,0:T(2,128)(2,1)}, bf16[128,1,7168]{2,1,0:T(2,128)(2,1)}) fusion(bf16[128,2,7168]{2,1,0:T(2,128)(2,1)} %reshape.117), kind=kLoop, calls=%fused_computation.53 | loop fusion | bytes 7340032 | tf_op jit(solution)/shard_map/slice | solution.py:61
  723.4 8.4 %copy.68 = bf16[128,1,7168]{0,2,1:T(8,128)(2,1)} copy(bf16[128,1,7168]{2,1,0:T(2,128)(2,1)} %get-tuple-element.7) | data formatting | bytes 3670016
  731.8 8.4 %copy.69 = bf16[128,1,7168]{0,2,1:T(8,128)(2,1)} copy(bf16[128,1,7168]{2,1,0:T(2,128)(2,1)} %get-tuple-element.8) | data formatting | bytes 3670016
  740.2 0.0 copy-start.1
  740.2 5.7 fusion.10
  745.9 3.9 copy.67
  749.8 0.0 copy-done.1
  (12 shorter events, 0.1 us)
Async XLA Ops:
  6.5 1.5 copy-start
  6.5 218.5 %all-gather.4.cloned.1.call-start = ((), (), s32[]{:S(2)}) async-start(), calls=%async_computation.3 | async-start | bytes 22020096 | tf_op jit(solution)/shard_map/all_gather | solution.py:45
  7.3 355.5 %all-gather.6.cloned.1.call-start = ((), (), s32[]{:S(2)}) async-start(), calls=%async_computation.4 | async-start | bytes 22020096 | tf_op jit(solution)/shard_map/all_gather | solution.py:46
  9.7 48.8 %all-to-all-start = ((bf16[16,128,448]{1,2,0:T(8,128)(2,1)}), bf16[16,128,448]{1,2,0:T(8,128)(2,1)S(1)}, u32[]{:S(2)}, u32[]{:S(2)}) async-start(bf16[16,128,448]{1,2,0:T(8,128)(2,1)} %copy_bitcast_fusion), calls=%async_computation | async-start | bytes 3670016 | tf_op jit(solution)/shard_map/all_to_all | solution.py:10
  16.3 0.7 copy-start.5
  16.3 523.6 %all-gather.8.cloned.1.call-start = ((), (), s32[]{:S(2)}) async-start(), calls=%async_computation.5 | async-start | bytes 22020096 | tf_op jit(solution)/shard_map/all_gather | solution.py:51
  17.1 4.6 copy-start.6
  58.5 7.1 copy-start.2
  58.5 3.2 copy-start.3
  561.1 6.8 copy-start.4
  561.1 127.1 %all-to-all-start.2 = ((bf16[16,20,7168]{2,1,0:T(8,128)(2,1)}), bf16[16,20,7168]{2,1,0:T(8,128)(2,1)}, u32[]{:S(2)}, u32[]{:S(2)}) async-start(bf16[16,20,7168]{2,1,0:T(8,128)(2,1)} %fusion.6), calls=%async_computation.2 | async-start | bytes 11010048 | tf_op jit(solution)/shard_map/all_to_all | solution.py:55
  740.2 9.6 %copy-start.1 = (bf16[2048,448]{0,1:T(8,128)(2,1)S(1)}, bf16[2048,448]{0,1:T(8,128)(2,1)}, u32[]{:S(2)}) copy-start(bf16[2048,448]{0,1:T(8,128)(2,1)} %param.8) | copy-start | bytes 5505028
Sparse Core Ops, SparseCore 0:
  8.9 176.6 all-gather.3
  187.2 175.5 all-gather.5
  364.3 175.5 all-gather.7
where the time goes:
time: 758 us; the launch traced here: 756 us
  waiting for transfers between devices  447 us (59%)
  blocking collectives  125 us (16%)
  local copies, waits for them, and re-layouts  99.3 us (13%)
  matrix products  44.7 us (6%)
  other arithmetic  13.6 us (2%)
  between operations  13.3 us (2%)
  starting transfers between devices  13.1 us (2%)
    all_gather x1, waiting for transfers between devices, body(): lax.all_gather(down_weight, 'blk', axis=1, tiled=True)  166 us
    all_gather x1, waiting for transfers between devices, body(): upward = project_in(lax.all_gather(up_weight, 'blk', axis=2, tiled=True))  127 us
    all_to_all x1, blocking collectives, body(): lax.all_to_all(outgoing.reshape(groups, exp_local * capacity, width), 'dp...  125 us
    all_to_all x1, waiting for transfers between devices, body(): lax.all_to_all(results, 'dp', split_axis=0, concat_axis=0, tiled=True)  116 us
    all_to_all x1, waiting for transfers between devices, body(): lax.all_to_all(attn_cols, 'dp', split_axis=0, concat_axis=1, tiled=True)  35.6 us
    dot_general x2, matrix products, project_in(): jnp.einsum('secd,edf->secf', arrived, piece, preferred_element_type=jnp.f...  21.6 us
    dot_general x1, matrix products, body(): jnp.einsum('secf,edf->secd', hidden, lax.all_gather(down_weight, 'blk', a...  21.2 us
    unnamed x18, local copies, waits for them, and re-layouts  21.2 us
  transfers between devices with their start and end apart: 5, of which 4 were waited for; matrix products, arithmetic and copies ran while one was open for 10% of the time, Pallas kernels for 0%

commit v1 on v0

v1 whole, which is shorter than its diff:
```python
import functools

import jax
import jax.numpy as jnp
from jax import lax
from jax.experimental import pallas as pl
from jax.experimental.pallas import tpu as pltpu
from jax.sharding import PartitionSpec as P

FOLD = 4
TURNS = 2
VMEM = 48 * 1024 * 1024
F32 = jnp.float32
BF16 = jnp.bfloat16


def dot(a, b):
    return lax.dot_general(a, b, (((1,), (0,)), ((), ())), preferred_element_type=F32)


def dot_nt(a, b):
    return lax.dot_general(a, b, (((1,), (1,)), ((), ())), preferred_element_type=F32)


def as_mask(cond):
    return jnp.where(cond, 1.0, 0.0).astype(BF16)


def pack_turn(base, turn, aux_ref, normed, slabs):
    tokens, width = normed.shape
    quarter = width // FOLD
    more = base // FOLD
    rows = len(slabs) * base
    row = lax.broadcasted_iota(jnp.int32, (rows, tokens), 0).astype(F32)
    at = 2 + 4 * turn
    whole = as_mask((row == aux_ref[at : at + 1, :]) | (row == aux_ref[at + 1 : at + 2, :]))
    folded = jnp.zeros((rows, quarter), F32)
    for k in range(FOLD):
        cols = slice(k * quarter, (k + 1) * quarter)
        block = dot(whole, normed[:, cols]).astype(BF16)
        for p, slab in enumerate(slabs):
            slab[:, cols] = block[p * base : (p + 1) * base]
        shift = row - k * more
        rest = (shift == aux_ref[at + 2 : at + 3, :]) | (shift == aux_ref[at + 3 : at + 4, :])
        folded += dot(as_mask(rest), normed[:, cols])
    folded = folded.astype(BF16)
    for p, slab in enumerate(slabs):
        slab[:, width:] = folded[p * base : (p + 1) * base]


def first_kernel(base, me_ref, attn_ref, res_ref, gain_ref, router_ref, ids_ref, aux_ref, normed_ref, *refs):
    slabs, held = refs[:-1], refs[-1]
    tokens, width = res_ref.shape
    experts = router_ref.shape[0]
    quarter = width // FOLD
    total = jnp.zeros((tokens, 1), F32)
    for k in range(FOLD):
        cols = slice(k * quarter, (k + 1) * quarter)
        part = res_ref[:, cols].astype(F32) + attn_ref[cols, :].astype(F32).T
        held[:, cols] = part
        total += jnp.sum(part * part, axis=1, keepdims=True)
    scale = lax.rsqrt(total / width + 1e-06)
    logits = jnp.zeros((experts, tokens), F32)
    for k in range(FOLD):
        cols = slice(k * quarter, (k + 1) * quarter)
        piece = (held[:, cols] * scale * gain_ref[:, cols].astype(F32)).astype(BF16)
        normed_ref[:, cols] = piece
        logits += dot_nt(router_ref[:, cols], piece)
    affinity = jax.nn.sigmoid(logits)
    expert = lax.broadcasted_iota(jnp.int32, (experts, tokens), 0)
    hit = [expert == ids_ref[k : k + 1, :] for k in range(2)]
    named = as_mask(hit[0] | hit[1])
    first = lax.broadcasted_iota(jnp.int32, (tokens, tokens), 0)
    second = lax.broadcasted_iota(jnp.int32, (tokens, tokens), 1)
    before = dot(named, as_mask(first < second))
    chosen = [jnp.sum(jnp.where(h, affinity, 0.0), axis=0, keepdims=True) for h in hit]
    ranks = [
        jnp.sum(jnp.where(h, before, 0.0), axis=0, keepdims=True).astype(jnp.int32) for h in hit
    ]
    denom = chosen[0] + chosen[1]
    aux_ref[...] = jnp.zeros_like(aux_ref)
    for k in range(2):
        aux_ref[k : k + 1, :] = 2.5 * chosen[k] / denom
        offset = ids_ref[k : k + 1, :] - me_ref[0]
        offset = jnp.where(offset < 0, offset + experts, offset)
        for turn in range(TURNS):
            here = offset % TURNS == turn
            row = offset // TURNS * base + ranks[k]
            at = 2 + 4 * turn + k
            main = jnp.where(here & (ranks[k] < base), row, -experts * base)
            rest = jnp.where(here & (ranks[k] >= base), row - base, -experts * base)
            aux_ref[at : at + 1, :] = main.astype(F32)
            aux_ref[at + 2 : at + 3, :] = rest.astype(F32)
    pack_turn(base, 0, aux_ref, normed_ref, slabs)


def first(base, me, attn, residual, gain, router, ids):
    tokens, width = residual.shape
    count = router.shape[0] // TURNS
    slab = jax.ShapeDtypeStruct((base, width + width // FOLD), BF16)
    return pl.pallas_call(
        functools.partial(first_kernel, base),
        in_specs=[pl.BlockSpec(memory_space=pltpu.SMEM)] + [pl.BlockSpec(memory_space=pltpu.VMEM)] * 5,
        out_shape=[
            jax.ShapeDtypeStruct((16, tokens), F32),
            jax.ShapeDtypeStruct((tokens, width), BF16),
        ]
        + [slab] * count,
        scratch_shapes=[pltpu.VMEM((tokens, width), F32)],
        compiler_params=pltpu.CompilerParams(vmem_limit_bytes=VMEM),
        cost_estimate=pl.CostEstimate(
            flops=2 * count * base * tokens * width,
            bytes_accessed=10 * tokens * width,
            transcendentals=0,
        ),
        name="first",
    )(me, attn, residual, gain, router, ids)


def others_kernel(base, turn, attn_ref, res_ref, aux_ref, normed_ref, stream_ref, *slabs):
    pack_turn(base, turn, aux_ref, normed_ref, slabs)
    width = res_ref.shape[1]
    quarter = width // FOLD
    for k in range(FOLD):
        cols = slice(k * quarter, (k + 1) * quarter)
        stream_ref[:, cols] = res_ref[:, cols].astype(F32) + attn_ref[cols, :].astype(F32).T


def others(base, turn, attn, residual, aux, normed, count):
    tokens, width = residual.shape
    slab = jax.ShapeDtypeStruct((base, width + width // FOLD), BF16)
    return pl.pallas_call(
        functools.partial(others_kernel, base, turn),
        out_shape=[jax.ShapeDtypeStruct((tokens, width), F32)] + [slab] * count,
        compiler_params=pltpu.CompilerParams(vmem_limit_bytes=VMEM),
        cost_estimate=pl.CostEstimate(
            flops=2 * count * base * tokens * width,
            bytes_accessed=12 * tokens * width,
            transcendentals=0,
        ),
        name="others",
    )(attn, residual, aux, normed)


def inward_kernel(base, *refs):
    slabs, (gate_ref, up_ref, out_ref, acc) = refs[:-4], refs[-4:]
    quarter, ff = gate_ref.shape[1:]
    more = base // FOLD
    rows = len(slabs) * base
    few = len(slabs) * more
    step = pl.program_id(0)

    @pl.when(step == 0)
    def _():
        acc[...] = jnp.zeros_like(acc)

    cols = pl.ds(pl.multiple_of(step * quarter, quarter), quarter)
    behind = jnp.concatenate([slab[:, quarter * FOLD :] for slab in slabs], axis=0)
    out_row = lax.broadcasted_iota(jnp.int32, (few, rows), 0)
    in_row = lax.broadcasted_iota(jnp.int32, (few, rows), 1)
    select = as_mask(in_row == (out_row // more) * base + step * more + out_row % more)
    rest = dot(select, behind).astype(BF16)
    block = jnp.concatenate([slab[:, cols] for slab in slabs] + [rest], axis=0)
    acc[:, :ff] += dot(block, gate_ref[0])
    acc[:, ff:] += dot(block, up_ref[0])

    @pl.when(step == FOLD - 1)
    def _():
        gated = acc[:, :ff]
        out_ref[...] = (gated / (1.0 + jnp.exp(-gated)) * acc[:, ff:]).astype(BF16)


def inward(base, slabs, gate, up):
    width, ff = gate.shape[1:]
    quarter = width // FOLD
    total = len(slabs) * (base + base // FOLD)
    return pl.pallas_call(
        functools.partial(inward_kernel, base),
        grid=(FOLD,),
        in_specs=[pl.BlockSpec(slabs[0].shape, lambda i: (0, 0))] * len(slabs)
        + [pl.BlockSpec((1, quarter, ff), lambda i: (0, i, 0))] * 2,
        out_specs=pl.BlockSpec((total, ff), lambda i: (0, 0)),
        out_shape=jax.ShapeDtypeStruct((total, ff), BF16),
        scratch_shapes=[pltpu.VMEM((total, 2 * ff), F32)],
        compiler_params=pltpu.CompilerParams(vmem_limit_bytes=VMEM),
        cost_estimate=pl.CostEstimate(flops=total, bytes_accessed=total, transcendentals=0),
        name="inward",
    )(*slabs, gate, up)


def outward_kernel(base, fold, parts, here_ref, *refs):
    hidden, down_ref, slabs, folded = refs[:parts], refs[parts], refs[parts + 1 : -1], refs[-1]
    step = pl.program_id(0)
    here = here_ref[0]
    more = base // FOLD
    rows = len(slabs) * base
    few = len(slabs) * more
    ff = hidden[0].shape[1]

    @pl.when(step == 0)
    def _():
        folded[...] = jnp.zeros_like(folded)

    @pl.when(step < fold)
    def _():
        made = None
        for o in range(parts):
            order = [(j - o) % parts for j in range(parts)]
            main, rest = rows // parts, few // parts
            block = jnp.concatenate(
                [hidden[o][i * main : (i + 1) * main, :] for i in order]
                + [hidden[o][rows + i * rest : rows + (i + 1) * rest, :] for i in order],
                axis=0,
            )
            at = pl.multiple_of(lax.rem(here + parts - o, parts) * ff, ff)
            term = dot_nt(block, down_ref[0, :, pl.ds(at, ff)])
            made = term if made is None else made + term
        made = made.astype(BF16)
        out_row = lax.broadcasted_iota(jnp.int32, (rows, few), 0)
        in_row = lax.broadcasted_iota(jnp.int32, (rows, few), 1)
        place = as_mask(out_row == (in_row // more) * base + step * more + in_row % more)
        for p, slab in enumerate(slabs):
            slab[...] = made[p * base : (p + 1) * base]
        folded[...] += dot(place, made[rows:])

    @pl.when(step == fold)
    def _():
        last = folded[...].astype(BF16)
        for p, slab in enumerate(slabs):
            slab[...] = last[p * base : (p + 1) * base]


def outward(base, fold, count, here, hidden, down):
    parts = len(hidden)
    total, ff = hidden[0].shape
    cols = down.shape[1]
    step = cols // fold
    return pl.pallas_call(
        functools.partial(outward_kernel, base, fold, parts),
        grid_spec=pltpu.PrefetchScalarGridSpec(
            num_scalar_prefetch=1,
            grid=(fold + 1,),
            in_specs=[pl.BlockSpec((total, ff), lambda i, here: (0, 0))] * parts
            + [pl.BlockSpec((1, step, parts * ff), lambda i, here: (0, jnp.minimum(i, fold - 1), 0))],
            out_specs=[pl.BlockSpec((base, step), lambda i, here: (0, i))] * count,
            scratch_shapes=[pltpu.VMEM((count * base, step), F32)],
        ),
        out_shape=[jax.ShapeDtypeStruct((base, cols + step), BF16)] * count,
        compiler_params=pltpu.CompilerParams(vmem_limit_bytes=VMEM),
        cost_estimate=pl.CostEstimate(flops=total, bytes_accessed=total, transcendentals=0),
        name="outward",
    )(here, *hidden, down)


def combine_kernel(base, fold, turn, parts, here_ref, aux_ref, stream_ref, *refs):
    slabs, out_ref = refs[:-1], refs[-1]
    count = len(slabs) // parts
    tokens = out_ref.shape[0]
    cols = out_ref.shape[1] // parts
    step = cols // fold
    more = base // FOLD
    row = lax.broadcasted_iota(jnp.int32, (count * base, tokens), 0).astype(F32)
    at = 2 + 4 * turn

    def matrix(start, shift):
        both = jnp.where(row - shift == aux_ref[start : start + 1, :], aux_ref[0:1, :], 0.0)
        both += jnp.where(row - shift == aux_ref[start + 1 : start + 2, :], aux_ref[1:2, :], 0.0)
        both = both.T
        high = both.astype(BF16)
        return high, (both - high.astype(F32)).astype(BF16)

    high, low = matrix(at, 0)
    rests = [matrix(at + 2, q * more) for q in range(fold)]
    for o in range(parts):
        start = lax.rem(here_ref[0] + o, parts) * cols
        back = jnp.concatenate([slab[...] for slab in slabs[o * count : (o + 1) * count]], axis=0)
        for q, (rest_high, rest_low) in enumerate(rests):
            main = back[:, q * step : (q + 1) * step]
            behind = back[:, cols:]
            total = dot(low, main) + dot(rest_low, behind)
            total += dot(high, main) + dot(rest_high, behind)
            cut = pl.ds(pl.multiple_of(start + q * step, step), step)
            out_ref[:, cut] = (stream_ref[:, cut] + total).astype(out_ref.dtype)


def combine(base, fold, turn, parts, here, aux, stream, slabs):
    tokens, width = stream.shape
    last = turn == TURNS - 1
    return pl.pallas_call(
        functools.partial(combine_kernel, base, fold, turn, parts),
        in_specs=[pl.BlockSpec(memory_space=pltpu.SMEM)]
        + [pl.BlockSpec(memory_space=pltpu.VMEM)] * (2 + len(slabs)),
        out_shape=jax.ShapeDtypeStruct((tokens, width), BF16 if last else F32),
        compiler_params=pltpu.CompilerParams(vmem_limit_bytes=VMEM),
        cost_estimate=pl.CostEstimate(
            flops=4 * tokens * width * len(slabs) // parts * base,
            bytes_accessed=8 * tokens * width,
            transcendentals=0,
        ),
        name="combine",
    )(here, aux, stream, *slabs)


def body(
    attn_cols, residual, norm_gain, router_weight, expert_ids, gate_weight, up_weight, down_weight
):
    groups = lax.axis_size("dp")
    parts = lax.axis_size("blk")
    tokens, width = residual.shape
    experts = router_weight.shape[1]
    fanout = expert_ids.shape[1]
    assert gate_weight.shape[0] == 1 and fanout == 2 and groups % TURNS == 0
    capacity = max(2, (5 * tokens * fanout + 4 * experts - 1) // (4 * experts))
    base = capacity * FOLD // (FOLD + 1)
    assert base * (FOLD + 1) == capacity * FOLD and base % FOLD == 0
    cols = down_weight.shape[1]
    fold = max(f for f in (1, 2, FOLD) if cols % (128 * f) == 0)
    count = groups // TURNS
    me = lax.axis_index("dp").astype(jnp.int32).reshape(1)
    here = lax.axis_index("blk").astype(jnp.int32).reshape(1)

    def across(block, shift):
        perm = [(i, (i + shift) % parts) for i in range(parts)]
        return lax.ppermute(block, "blk", perm) if shift else block

    def forth(slab, offset):
        perm = [(i, (i + offset) % groups) for i in range(groups)]
        return lax.ppermute(slab, "dp", perm) if offset else slab

    def back(slab, offset, shift):
        perm = [
            (i * parts + j, (i - offset) % groups * parts + (j - shift) % parts)
            for i in range(groups)
            for j in range(parts)
        ]
        return lax.ppermute(slab, ("dp", "blk"), perm) if offset or shift else slab

    held = attn_cols.shape[1]
    send = attn_cols.T.reshape(held, groups, tokens).transpose(1, 0, 2)
    attn = lax.all_to_all(send, "dp", split_axis=0, concat_axis=0, tiled=True)
    attn = attn.reshape(width, tokens)
    aux, normed, *slabs = first(
        base, me, attn, residual, norm_gain.reshape(1, width), router_weight.T, expert_ids.T
    )
    stream, *rest = others(base, 1, attn, residual, aux, normed, count)
    arrived = []
    for turn, packs in enumerate((slabs, rest)):
        own = [None] * count
        for p in sorted(range(count), key=lambda p: abs(TURNS * p + turn - groups // 2)):
            own[p] = forth(packs[p], TURNS * p + turn)
        arrived.append([across(slab, o) for o in range(parts) for slab in own])
    returned = None
    for turn in range(TURNS):
        if returned is not None:
            half = len(returned) // 2
            arrived[turn], returned[:half] = lax.optimization_barrier(
                (arrived[turn], returned[:half])
            )
        hidden = inward(base, arrived[turn], gate_weight, up_weight)
        hidden = [across(hidden, o) for o in range(parts)]
        made = outward(base, fold, count * parts, here, hidden, down_weight)
        returned = [
            back(made[o * count + p], TURNS * p + turn, o)
            for o in range(parts)
            for p in range(count)
        ]
        if turn == 0:
            ready = returned
    stream = combine(base, fold, 0, parts, here, aux, stream, ready)
    return combine(base, fold, 1, parts, here, aux, stream, returned)


def solution(mesh):
    return jax.shard_map(
        body,
        mesh=mesh,
        in_specs=(
            P("blk", "dp"),
            P(("blk", "dp"), None),
            P(),
            P(),
            P(("blk", "dp"), None),
            P("dp", None, "blk"),
            P("dp", None, "blk"),
            P("dp", "blk", None),
        ),
        out_specs=P(("blk", "dp"), None),
        check_vma=False,
    )
```

time: 758 us -> 368 us (0.49)
  waiting for transfers between devices: 447 us -> 191 us
  blocking collectives: 125 us -> 0 us
  starting transfers between devices: 13.1 us -> 117 us
  local copies, waits for them, and re-layouts: 99.3 us -> 6.66 us
  Pallas kernels: 0 us -> 50.6 us
  matrix products: 44.7 us -> 0 us
  other arithmetic: 13.6 us -> 0 us
  between operations: 13.3 us -> 0.21 us
    all_gather x3 -> x0, waiting for transfers between devices: 293 us -> none  [the longest x1 166 us: body(): lax.all_gather(down_weight, 'blk', axis=1, tiled=True)]
    ppermute x0 -> x64, waiting for transfers between devices: none -> 149 us  [the longest x18 65.5 us: across(): return lax.ppermute(block, 'blk', perm) if shift else block]
    all_to_all x1 -> x0, blocking collectives: 125 us -> none  [body(): lax.all_to_all(outgoing.reshape(groups, exp_local * capacity, width), 'dp...]
    ppermute x0 -> x64, starting transfers between devices: none -> 110 us  [the longest x31 82.9 us: back(): return lax.ppermute(slab, ('dp', 'blk'), perm) if offset or shift else slab]
    all_to_all x2 -> x1, waiting for transfers between devices: 152 us -> 41.9 us  [body(): attn = lax.all_to_all(send, 'dp', split_axis=0, concat_axis=0, tiled=True)]
    pallas_call x0 -> x8, Pallas kernels: none -> 50.6 us  [the longest x2 19 us: inward(): pl.pallas_call(functools.partial(inward_kernel, base), grid=(FOLD,), in_s...]
    dot_general x4 -> x0, matrix products: 44.7 us -> none  [the longest x2 21.6 us: project_in(): jnp.einsum('secd,edf->secf', arrived, piece, preferred_element_type=jnp.f...]
    reshape x4 -> x1, local copies, waits for them, and re-layouts: 31.1 us -> 0.02 us  [body(): norm_gain.reshape(1, width)]
  transfers between devices with their start and end apart: 5 -> 65, of which waited for: 4 -> 24; matrix products, arithmetic and copies ran while one was open for 10% -> 0% of each run, Pallas kernels for 0% -> 9%
where the time goes in v1:
time: 368 us; the launch traced here: 365 us
  waiting for transfers between devices  191 us (52%)
  starting transfers between devices  117 us (32%)
  Pallas kernels  50.6 us (14%)
  local copies, waits for them, and re-layouts  6.66 us (2%)
    ppermute x31, starting transfers between devices, back(): return lax.ppermute(slab, ('dp', 'blk'), perm) if offset or shift else slab  82.9 us
    ppermute x18, waiting for transfers between devices, across(): return lax.ppermute(block, 'blk', perm) if shift else block  65.5 us
    ppermute x15, waiting for transfers between devices, forth(): return lax.ppermute(slab, 'dp', perm) if offset else slab  64.9 us
    all_to_all x1, waiting for transfers between devices, body(): attn = lax.all_to_all(send, 'dp', split_axis=0, concat_axis=0, tiled=True)  41.9 us
    pallas_call x2, Pallas kernels, inward(): pl.pallas_call(functools.partial(inward_kernel, base), grid=(FOLD,), in_s...  19 us
    ppermute x31, waiting for transfers between devices, back(): return lax.ppermute(slab, ('dp', 'blk'), perm) if offset or shift else slab  18.8 us
    ppermute x15, starting transfers between devices, forth(): return lax.ppermute(slab, 'dp', perm) if offset else slab  15.3 us
    pallas_call x2, Pallas kernels, outward(): pl.pallas_call(functools.partial(outward_kernel, base, fold, parts), grid...  14.1 us
  transfers between devices with their start and end apart: 65, of which 24 were waited for; matrix products, arithmetic and copies ran while one was open for 0% of the time, Pallas kernels for 9%

profile of v1, /device:TPU:11, one launch (start us, length us, event | category | flops | bytes accessed | tf_op | source)
XLA Modules:
  0.0 365.1 jit_solution(5062376422615743766)
XLA Ops:
  0.0 1.5 copy-done
  1.5 1.7 bitcast_bitcast_fusion
  3.2 6.7 %all-to-all-start = ((bf16[16,448,128]{2,1,0:T(8,128)(2,1)}), bf16[16,448,128]{2,1,0:T(8,128)(2,1)}, u32[]{:S(2)}, u32[]{:S(2)}) async-start(bf16[16,448,128]{2,1,0:T(8,128)(2,1)} %bitcast_bitcast_fusion), calls=%async_computation | async-start | bytes 3670016 | tf_op jit(solution)/shard_map/all_to_all | solution.py:340
  9.9 41.9 %all-to-all-done = bf16[16,448,128]{2,1,0:T(8,128)(2,1)} async-done(((bf16[16,448,128]{2,1,0:T(8,128)(2,1)}), bf16[16,448,128]{2,1,0:T(8,128)(2,1)}, u32[]{:S(2)}, u32[]{:S(2)}) %all-to-all-start) | async-done | bytes 1835040 | tf_op jit(solution)/shard_map/all_to_all | solution.py:340
  51.8 4.7 %first.1 = (f32[16,128]{1,0:T(8,128)S(1)}, bf16[128,7168]{1,0:T(8,128)(2,1)S(1)}, bf16[16,8960]{1,0:T(8,128)(2,1)S(1)}, bf16[16,8960]{1,0:T(8,128)(2,1)S(1)}, bf...) custom-call(s32[1]{0:T(128)} %bitcast.1.me_ref, ...), custom_call_target="tpu_custom_call" | custom-call | flops 234881024 | bytes 9175040 | tf_op jit(solution)/shard_map/first/pallas_call | solution.py:101
  58.6 1.4 collective-permute-start.18
  60.0 1.2 collective-permute-start.19
  61.3 1.3 collective-permute-start.20
  62.6 3.4 collective-permute-done.16.refs_1_
  66.0 5.4 %collective-permute-done.17.refs_2_ = bf16[16,8960]{1,0:T(8,128)(2,1)S(1)} collective-permute-done((bf16[16,8960]{1,0:T(8,128)(2,1)S(1)}, bf16[16,8960]{1,0:T(8,128)(2,1)S(1)}, u32[]{:S(2)}, u32[]{:S(2)}) %collective-permute-start.17) | collective-permute-done | bytes 286752 | tf_op jit(solution)/shard_map/ppermute | solution.py:328
  71.4 29.4 %collective-permute-done.18.refs_3_ = bf16[16,8960]{1,0:T(8,128)(2,1)S(1)} collective-permute-done((bf16[16,8960]{1,0:T(8,128)(2,1)S(1)}, bf16[16,8960]{1,0:T(8,128)(2,1)S(1)}, u32[]{:S(2)}, u32[]{:S(2)}) %collective-permute-start.18) | collective-permute-done | bytes 286752 | tf_op jit(solution)/shard_map/ppermute | solution.py:328
  100.8 1.2 collective-permute-start.23
  102.0 5.1 %others.1 = (f32[128,7168]{1,0:T(8,128)}, bf16[16,8960]{1,0:T(8,128)(2,1)S(1)}, bf16[16,8960]{1,0:T(8,128)(2,1)S(1)}, bf16[16,8960]{1,0:T(8,128)(2,1)S(1)}, bf16...) custom-call(bf16[7168,128]{1,0:T(8,128)(2,1)} %bitcast.4.attn_ref, ...), custom_call_target="tpu_custom_call" | custom-call | flops 234881024 | bytes 11010048 | tf_op jit(solution)/shard_map/others/pallas_call | solution.py:132
  107.2 7.3 %collective-permute-start.2 = (bf16[16,8960]{1,0:T(8,128)(2,1)S(1)}, bf16[16,8960]{1,0:T(8,128)(2,1)S(1)}, u32[]{:S(2)}, u32[]{:S(2)}) collective-permute-start(bf16[16,8960]{1,0:T(8,128)(2,1)S(1)} %get-tuple-element.85), channel_id=1, source_target_pairs={{0,10},{2,12},{4,14},{6,16},{8,18},{10,20},{12,22},{14,24},{16,26}... | collective-permute-start | bytes 860168 | tf_op jit(solution)/shard_map/ppermute | solution.py:328
  114.5 2.6 collective-permute-start.4
  118.3 20.5 %collective-permute-done.2.refs_2_ = bf16[16,8960]{1,0:T(8,128)(2,1)S(1)} collective-permute-done((bf16[16,8960]{1,0:T(8,128)(2,1)S(1)}, bf16[16,8960]{1,0:T(8,128)(2,1)S(1)}, u32[]{:S(2)}, u32[]{:S(2)}) %collective-permute-start.2) | collective-permute-done | bytes 286752 | tf_op jit(solution)/shard_map/ppermute | solution.py:328
  138.9 6.1 %collective-permute-done.3.refs_3_ = bf16[16,8960]{1,0:T(8,128)(2,1)S(1)} collective-permute-done((bf16[16,8960]{1,0:T(8,128)(2,1)S(1)}, bf16[16,8960]{1,0:T(8,128)(2,1)S(1)}, u32[]{:S(2)}, u32[]{:S(2)}) %collective-permute-start.3) | collective-permute-done | bytes 286752 | tf_op jit(solution)/shard_map/ppermute | solution.py:328
  145.0 1.4 collective-permute-start.27
  146.5 1.4 collective-permute-start.29
  148.0 3.9 %collective-permute-done.26.refs_11_ = bf16[16,8960]{1,0:T(8,128)(2,1)S(1)} collective-permute-done((bf16[16,8960]{1,0:T(8,128)(2,1)S(1)}, bf16[16,8960]{1,0:T(8,128)(2,1)S(1)}, u32[]{:S(2)}, u32[]{:S(2)}) %collective-permute-start.26) | collective-permute-done | bytes 286752 | tf_op jit(solution)/shard_map/ppermute | solution.py:324
  152.5 5.7 %collective-permute-done.27.refs_12_ = bf16[16,8960]{1,0:T(8,128)(2,1)S(1)} collective-permute-done((bf16[16,8960]{1,0:T(8,128)(2,1)S(1)}, bf16[16,8960]{1,0:T(8,128)(2,1)S(1)}, u32[]{:S(2)}, u32[]{:S(2)}) %collective-permute-start.27) | collective-permute-done | bytes 286752 | tf_op jit(solution)/shard_map/ppermute | solution.py:324
  158.2 6.0 %collective-permute-done.28.refs_13_ = bf16[16,8960]{1,0:T(8,128)(2,1)S(1)} collective-permute-done((bf16[16,8960]{1,0:T(8,128)(2,1)S(1)}, bf16[16,8960]{1,0:T(8,128)(2,1)S(1)}, u32[]{:S(2)}, u32[]{:S(2)}) %collective-permute-start.28) | collective-permute-done | bytes 286752 | tf_op jit(solution)/shard_map/ppermute | solution.py:324
  164.2 6.1 %collective-permute-done.29.refs_14_ = bf16[16,8960]{1,0:T(8,128)(2,1)S(1)} collective-permute-done((bf16[16,8960]{1,0:T(8,128)(2,1)S(1)}, bf16[16,8960]{1,0:T(8,128)(2,1)S(1)}, u32[]{:S(2)}, u32[]{:S(2)}) %collective-permute-start.29) | collective-permute-done | bytes 286752 | tf_op jit(solution)/shard_map/ppermute | solution.py:324
  170.4 5.2 %collective-permute-done.30.refs_15_ = bf16[16,8960]{1,0:T(8,128)(2,1)S(1)} collective-permute-done((bf16[16,8960]{1,0:T(8,128)(2,1)S(1)}, bf16[16,8960]{1,0:T(8,128)(2,1)S(1)}, u32[]{:S(2)}, u32[]{:S(2)}) %collective-permute-start.30) | collective-permute-done | bytes 286752 | tf_op jit(solution)/shard_map/ppermute | solution.py:324
  175.6 1.2 collective-permute-start.10
  176.8 9.1 %inward.2.refs_0_ = bf16[320,512]{1,0:T(8,128)(2,1)S(1)} custom-call(bf16[16,8960]{1,0:T(8,128)(2,1)S(1)} %get-tuple-element.91.refs_0_, bf16[16,8960]{1,0:T(8,128)(2,1)S(1)} %collective-permute-done.16.refs_1_, bf16[16,8960]{1,0:T(8,128)(2,1)S(1)} %collective-permute-done.17.refs_2_, bf16[16,8960]{1,0:T(8,128)(2,1)S(1)} %collective-permute-done.18.refs_3_, ...), custom_call_target="tpu_custom_call" | custom-call | flops 320 | bytes 320 | tf_op jit(solution)/shard_map/inward/pallas_call | solution.py:177
  186.2 1.2 collective-permute-start.11
  187.7 1.2 collective-permute-start.13
  189.8 12.0 %collective-permute-done.11.refs_11_ = bf16[16,8960]{1,0:T(8,128)(2,1)S(1)} collective-permute-done((bf16[16,8960]{1,0:T(8,128)(2,1)S(1)}, bf16[16,8960]{1,0:T(8,128)(2,1)S(1)}, u32[]{:S(2)}, u32[]{:S(2)}) %collective-permute-start.11) | collective-permute-done | bytes 286752 | tf_op jit(solution)/shard_map/ppermute | solution.py:324
  202.8 5.3 %collective-permute-done.12.refs_12_ = bf16[16,8960]{1,0:T(8,128)(2,1)S(1)} collective-permute-done((bf16[16,8960]{1,0:T(8,128)(2,1)S(1)}, bf16[16,8960]{1,0:T(8,128)(2,1)S(1)}, u32[]{:S(2)}, u32[]{:S(2)}) %collective-permute-start.12) | collective-permute-done | bytes 286752 | tf_op jit(solution)/shard_map/ppermute | solution.py:324
  210.3 7.1 %outward.2 = (bf16[16,4480]{1,0:T(8,128)(2,1)S(1)}, bf16[16,4480]{1,0:T(8,128)(2,1)S(1)}, bf16[16,4480]{1,0:T(8,128)(2,1)S(1)}, bf16[16,4480]{1,0:T(8,128)(2,1)S...) custom-call(s32[1]{0:T(128)} %bitcast.here_ref, ...), custom_call_target="tpu_custom_call" | custom-call | flops 320 | bytes 320 | tf_op jit(solution)/shard_map/outward/pallas_call | solution.py:238
  217.5 2.9 collective-permute-done.14.refs_14_
  220.4 6.1 %collective-permute-done.15.refs_15_ = bf16[16,8960]{1,0:T(8,128)(2,1)} collective-permute-done((bf16[16,8960]{1,0:T(8,128)(2,1)}, bf16[16,8960]{1,0:T(8,128)(2,1)}, u32[]{:S(2)}, u32[]{:S(2)}) %collective-permute-start.15) | collective-permute-done | bytes 286752 | tf_op jit(solution)/shard_map/ppermute | solution.py:324
  226.5 6.1 %collective-permute-done.8.refs_8_ = bf16[16,8960]{1,0:T(8,128)(2,1)} collective-permute-done((bf16[16,8960]{1,0:T(8,128)(2,1)}, bf16[16,8960]{1,0:T(8,128)(2,1)}, u32[]{:S(2)}, u32[]{:S(2)}) %collective-permute-start.8) | collective-permute-done | bytes 286752 | tf_op jit(solution)/shard_map/ppermute | solution.py:324
  232.7 6.0 %collective-permute-done.9.refs_9_ = bf16[16,8960]{1,0:T(8,128)(2,1)} collective-permute-done((bf16[16,8960]{1,0:T(8,128)(2,1)}, bf16[16,8960]{1,0:T(8,128)(2,1)}, u32[]{:S(2)}, u32[]{:S(2)}) %collective-permute-start.9) | collective-permute-done | bytes 286752 | tf_op jit(solution)/shard_map/ppermute | solution.py:324
  238.7 2.1 collective-permute-start.36
  241.0 2.6 collective-permute-done.35.refs_4_
  243.6 3.1 collective-permute-done.36.refs_5_
  246.7 3.1 collective-permute-done.37.refs_6_
  249.8 3.1 collective-permute-done.38.refs_7_
  252.9 9.9 %inward.3.refs_0_ = bf16[320,512]{1,0:T(8,128)(2,1)S(1)} custom-call(bf16[16,8960]{1,0:T(8,128)(2,1)} %collective-permute-done.refs_0_, bf16[16,8960]{1,0:T(8,128)(2,1)} %collective-permute-done.1.refs_1_, bf16[16,8960]{1,0:T(8,128)(2,1)S(1)} %collective-permute-done.2.refs_2_, bf16[16,8960]{1,0:T(8,128)(2,1)S(1)} %collective-permute-done.3.refs_3_, ...), custom_call_target="tpu_custom_call" | custom-call | flops 320 | bytes 320 | tf_op jit(solution)/shard_map/inward/pallas_call | solution.py:177
  262.9 1.5 collective-permute-start.39
  264.3 5.8 %collective-permute-start.40 = (bf16[16,4480]{1,0:T(8,128)(2,1)S(1)}, bf16[16,4480]{1,0:T(8,128)(2,1)S(1)}, u32[]{:S(2)}, u32[]{:S(2)}) collective-permute-start(bf16[16,4480]{1,0:T(8,128)(2,1)S(1)} %get-tuple-element.116), channel_id=1, source_target_pairs={{0,29},{1,28},{2,31},{3,30},{4,1},{5,0},{6,3},{7,2},{8,5},{9,4},{1... | collective-permute-start | bytes 430088 | tf_op jit(solution)/shard_map/ppermute | solution.py:336
  271.3 3.0 collective-permute-start.42
  274.6 7.0 %outward.3 = (bf16[16,4480]{1,0:T(8,128)(2,1)S(1)}, bf16[16,4480]{1,0:T(8,128)(2,1)S(1)}, bf16[16,4480]{1,0:T(8,128)(2,1)S(1)}, bf16[16,4480]{1,0:T(8,128)(2,1)S...) custom-call(s32[1]{0:T(128)} %bitcast.here_ref, ...), custom_call_target="tpu_custom_call" | custom-call | flops 320 | bytes 320 | tf_op jit(solution)/shard_map/outward/pallas_call | solution.py:238
  281.6 3.0 collective-permute-start.44
  284.6 3.1 collective-permute-start.45
  287.9 11.4 %collective-permute-start.48 = (bf16[16,4480]{1,0:T(8,128)(2,1)S(1)}, bf16[16,4480]{1,0:T(8,128)(2,1)S(1)}, u32[]{:S(2)}, u32[]{:S(2)}) collective-permute-start(bf16[16,4480]{1,0:T(8,128)(2,1)S(1)} %get-tuple-element.139), channel_id=1, source_target_pairs={{0,30},{1,31},{2,0},{3,1},{4,2},{5,3},{6,4},{7,5},{8,6},{9,7},{10,... | collective-permute-start | bytes 430088 | tf_op jit(solution)/shard_map/ppermute | solution.py:336
  299.3 2.5 collective-permute-start.49
  301.8 6.0 %collective-permute-start.51 = (bf16[16,4480]{1,0:T(8,128)(2,1)S(1)}, bf16[16,4480]{1,0:T(8,128)(2,1)S(1)}, u32[]{:S(2)}, u32[]{:S(2)}) collective-permute-start(bf16[16,4480]{1,0:T(8,128)(2,1)S(1)} %get-tuple-element.142), channel_id=1, source_target_pairs={{0,18},{1,19},{2,20},{3,21},{4,22},{5,23},{6,24},{7,25},{8,26},{9,... | collective-permute-start | bytes 430088 | tf_op jit(solution)/shard_map/ppermute | solution.py:336
  308.9 1.7 collective-permute-start.53
  310.6 8.1 %collective-permute-start.54 = (bf16[16,4480]{1,0:T(8,128)(2,1)S(1)}, bf16[16,4480]{1,0:T(8,128)(2,1)S(1)}, u32[]{:S(2)}, u32[]{:S(2)}) collective-permute-start(bf16[16,4480]{1,0:T(8,128)(2,1)S(1)} %get-tuple-element.145), channel_id=1, source_target_pairs={{0,6},{1,7},{2,8},{3,9},{4,10},{5,11},{6,12},{7,13},{8,14},{9,15},... | collective-permute-start | bytes 430088 | tf_op jit(solution)/shard_map/ppermute | solution.py:336
  318.7 3.7 collective-permute-start.55
  322.4 6.7 %collective-permute-start.56 = (bf16[16,4480]{1,0:T(8,128)(2,1)S(1)}, bf16[16,4480]{1,0:T(8,128)(2,1)S(1)}, u32[]{:S(2)}, u32[]{:S(2)}) collective-permute-start(bf16[16,4480]{1,0:T(8,128)(2,1)S(1)} %get-tuple-element.147), channel_id=1, source_target_pairs={{0,31},{1,30},{2,1},{3,0},{4,3},{5,2},{6,5},{7,4},{8,7},{9,6},{10,... | collective-permute-start | bytes 430088 | tf_op jit(solution)/shard_map/ppermute | solution.py:336
  329.0 1.4 collective-permute-start.57
  330.5 3.1 collective-permute-start.58
  333.5 1.4 collective-permute-start.59
  334.9 2.2 collective-permute-start.60
  337.1 3.2 collective-permute-start.61
  340.3 2.7 collective-permute-done.58.refs_10_
  342.9 10.2 %collective-permute-start.63 = (bf16[16,4480]{1,0:T(8,128)(2,1)S(1)}, bf16[16,4480]{1,0:T(8,128)(2,1)S(1)}, u32[]{:S(2)}, u32[]{:S(2)}) collective-permute-start(bf16[16,4480]{1,0:T(8,128)(2,1)S(1)} %get-tuple-element.154), channel_id=1, source_target_pairs={{0,3},{1,2},{2,5},{3,4},{4,7},{5,6},{6,9},{7,8},{8,11},{9,10},{10,... | collective-permute-start | bytes 430088 | tf_op jit(solution)/shard_map/ppermute | solution.py:336
  353.1 4.3 %combine.2.stream_ref = f32[128,7168]{1,0:T(8,128)S(1)} custom-call(s32[1]{0:T(128)} %bitcast.here_ref, f32[16,128]{1,0:T(8,128)S(1)} %get-tuple-element.80.aux_ref, f32[128,7168]{1,0:T(8,128)} %get-tuple-element.82.stream_ref, bf16[16,4480]{1,0:T(8,128)(2,1)S(1)} %get-tuple-element.107.refs_0_, bf16[16,4480]{1,0:T(8,128)(2,1)S(1)} %collective-permute-done.32.refs_1_, ...), custom_call_target="tpu_custom_call" | custom-call | flops 469762048 | bytes 7340032 | tf_op jit(solution)/shard_map/combine/pallas_call | solution.py:289
  358.6 3.1 collective-permute-done.63.refs_15_
  361.7 3.5 combine.3
  (100 shorter events, 13.1 us)
Async XLA Ops:
  3.2 48.6 %all-to-all-start = ((bf16[16,448,128]{2,1,0:T(8,128)(2,1)}), bf16[16,448,128]{2,1,0:T(8,128)(2,1)}, u32[]{:S(2)}, u32[]{:S(2)}) async-start(bf16[16,448,128]{2,1,0:T(8,128)(2,1)} %bitcast_bitcast_fusion), calls=%async_computation | async-start | bytes 3670016 | tf_op jit(solution)/shard_map/all_to_all | solution.py:340
  57.7 8.2 %collective-permute-start.16 = (bf16[16,8960]{1,0:T(8,128)(2,1)S(1)}, bf16[16,8960]{1,0:T(8,128)(2,1)S(1)}, u32[]{:S(2)}, u32[]{:S(2)}) collective-permute-start(bf16[16,8960]{1,0:T(8,128)(2,1)S(1)} %get-tuple-element.92), channel_id=1, source_target_pairs={{0,4},{2,6},{4,8},{6,10},{8,12},{10,14},{12,16},{14,18},{16,20},{1... | collective-permute-start | bytes 860168 | tf_op jit(solution)/shard_map/ppermute | solution.py:328
  58.6 12.7 %collective-permute-start.17 = (bf16[16,8960]{1,0:T(8,128)(2,1)S(1)}, bf16[16,8960]{1,0:T(8,128)(2,1)S(1)}, u32[]{:S(2)}, u32[]{:S(2)}) collective-permute-start(bf16[16,8960]{1,0:T(8,128)(2,1)S(1)} %get-tuple-element.93), channel_id=1, source_target_pairs={{0,8},{2,10},{4,12},{6,14},{8,16},{10,18},{12,20},{14,22},{16,24},... | collective-permute-start | bytes 860168 | tf_op jit(solution)/shard_map/ppermute | solution.py:328
  58.6 42.1 %collective-permute-start.18 = (bf16[16,8960]{1,0:T(8,128)(2,1)S(1)}, bf16[16,8960]{1,0:T(8,128)(2,1)S(1)}, u32[]{:S(2)}, u32[]{:S(2)}) collective-permute-start(bf16[16,8960]{1,0:T(8,128)(2,1)S(1)} %get-tuple-element.94), channel_id=1, source_target_pairs={{0,12},{2,14},{4,16},{6,18},{8,20},{10,22},{12,24},{14,26},{16,28}... | collective-permute-start | bytes 860168 | tf_op jit(solution)/shard_map/ppermute | solution.py:328
  60.0 47.1 %collective-permute-start.19 = (bf16[16,8960]{1,0:T(8,128)(2,1)S(1)}, bf16[16,8960]{1,0:T(8,128)(2,1)S(1)}, u32[]{:S(2)}, u32[]{:S(2)}) collective-permute-start(bf16[16,8960]{1,0:T(8,128)(2,1)S(1)} %get-tuple-element.95), channel_id=1, source_target_pairs={{0,16},{2,18},{4,20},{6,22},{8,24},{10,26},{12,28},{14,30},{16,0},... | collective-permute-start | bytes 860168 | tf_op jit(solution)/shard_map/ppermute | solution.py:328
  61.3 53.2 %collective-permute-start.20 = (bf16[16,8960]{1,0:T(8,128)(2,1)S(1)}, bf16[16,8960]{1,0:T(8,128)(2,1)S(1)}, u32[]{:S(2)}, u32[]{:S(2)}) collective-permute-start(bf16[16,8960]{1,0:T(8,128)(2,1)S(1)} %get-tuple-element.96), channel_id=1, source_target_pairs={{0,20},{2,22},{4,24},{6,26},{8,28},{10,30},{12,0},{14,2},{16,4},{1... | collective-permute-start | bytes 860168 | tf_op jit(solution)/shard_map/ppermute | solution.py:328
  66.0 48.5 %collective-permute-start.21 = (bf16[16,8960]{1,0:T(8,128)(2,1)S(1)}, bf16[16,8960]{1,0:T(8,128)(2,1)S(1)}, u32[]{:S(2)}, u32[]{:S(2)}) collective-permute-start(bf16[16,8960]{1,0:T(8,128)(2,1)S(1)} %get-tuple-element.97), channel_id=1, source_target_pairs={{0,24},{2,26},{4,28},{6,30},{8,0},{10,2},{12,4},{14,6},{16,8},{18,... | collective-permute-start | bytes 860168 | tf_op jit(solution)/shard_map/ppermute | solution.py:328
  71.4 45.7 %collective-permute-start.22 = (bf16[16,8960]{1,0:T(8,128)(2,1)S(1)}, bf16[16,8960]{1,0:T(8,128)(2,1)S(1)}, u32[]{:S(2)}, u32[]{:S(2)}) collective-permute-start(bf16[16,8960]{1,0:T(8,128)(2,1)S(1)} %get-tuple-element.98), channel_id=1, source_target_pairs={{0,28},{2,30},{4,0},{6,2},{8,4},{10,6},{12,8},{14,10},{16,12},{18,... | collective-permute-start | bytes 860168 | tf_op jit(solution)/shard_map/ppermute | solution.py:328
  100.8 16.4 %collective-permute-start.23 = (bf16[16,8960]{1,0:T(8,128)(2,1)S(1)}, bf16[16,8960]{1,0:T(8,128)(2,1)S(1)}, u32[]{:S(2)}, u32[]{:S(2)}) collective-permute-start(bf16[16,8960]{1,0:T(8,128)(2,1)S(1)} %get-tuple-element.91.refs_0_), channel_id=1, source_target_pairs={{0,1},{1,0},{2,3},{3,2},{4,5},{5,4},{6,7},{7,6},{8,9},{9,8},{10,11... | collective-permute-start | bytes 860168 | tf_op jit(solution)/shard_map/ppermute | solution.py:324
  107.2 31.7 %collective-permute-start.2 = (bf16[16,8960]{1,0:T(8,128)(2,1)S(1)}, bf16[16,8960]{1,0:T(8,128)(2,1)S(1)}, u32[]{:S(2)}, u32[]{:S(2)}) collective-permute-start(bf16[16,8960]{1,0:T(8,128)(2,1)S(1)} %get-tuple-element.85), channel_id=1, source_target_pairs={{0,10},{2,12},{4,14},{6,16},{8,18},{10,20},{12,22},{14,24},{16,26}... | collective-permute-start | bytes 860168 | tf_op jit(solution)/shard_map/ppermute | solution.py:328
  114.5 30.5 %collective-permute-start.3 = (bf16[16,8960]{1,0:T(8,128)(2,1)S(1)}, bf16[16,8960]{1,0:T(8,128)(2,1)S(1)}, u32[]{:S(2)}, u32[]{:S(2)}) collective-permute-start(bf16[16,8960]{1,0:T(8,128)(2,1)S(1)} %get-tuple-element.86), channel_id=1, source_target_pairs={{0,14},{2,16},{4,18},{6,20},{8,22},{10,24},{12,26},{14,28},{16,30}... | collective-permute-start | bytes 860168 | tf_op jit(solution)/shard_map/ppermute | solution.py:328
  114.5 30.6 %collective-permute-start.4 = (bf16[16,8960]{1,0:T(8,128)(2,1)S(1)}, bf16[16,8960]{1,0:T(8,128)(2,1)S(1)}, u32[]{:S(2)}, u32[]{:S(2)}) collective-permute-start(bf16[16,8960]{1,0:T(8,128)(2,1)S(1)} %get-tuple-element.87), channel_id=1, source_target_pairs={{0,18},{2,20},{4,22},{6,24},{8,26},{10,28},{12,30},{14,0},{16,2},{... | collective-permute-start | bytes 860168 | tf_op jit(solution)/shard_map/ppermute | solution.py:328
  117.1 29.4 %collective-permute-start.5 = (bf16[16,8960]{1,0:T(8,128)(2,1)S(1)}, bf16[16,8960]{1,0:T(8,128)(2,1)}, u32[]{:S(2)}, u32[]{:S(2)}) collective-permute-start(bf16[16,8960]{1,0:T(8,128)(2,1)S(1)} %get-tuple-element.88), channel_id=1, source_target_pairs={{0,22},{2,24},{4,26},{6,28},{8,30},{10,0},{12,2},{14,4},{16,6},{18... | collective-permute-start | bytes 860168 | tf_op jit(solution)/shard_map/ppermute | solution.py:328
  117.1 29.4 %collective-permute-start.24 = (bf16[16,8960]{1,0:T(8,128)(2,1)S(1)}, bf16[16,8960]{1,0:T(8,128)(2,1)S(1)}, u32[]{:S(2)}, u32[]{:S(2)}) collective-permute-start(bf16[16,8960]{1,0:T(8,128)(2,1)S(1)} %collective-permute-done.16.refs_1_), channel_id=1, source_target_pairs={{0,1},{1,0},{2,3},{3,2},{4,5},{5,4},{6,7},{7,6},{8,9},{9,8},{10,11... | collective-permute-start | bytes 860168 | tf_op jit(solution)/shard_map/ppermute | solution.py:324
  138.9 9.1 %collective-permute-start.25 = (bf16[16,8960]{1,0:T(8,128)(2,1)S(1)}, bf16[16,8960]{1,0:T(8,128)(2,1)S(1)}, u32[]{:S(2)}, u32[]{:S(2)}) collective-permute-start(bf16[16,8960]{1,0:T(8,128)(2,1)S(1)} %collective-permute-done.17.refs_2_), channel_id=1, source_target_pairs={{0,1},{1,0},{2,3},{3,2},{4,5},{5,4},{6,7},{7,6},{8,9},{9,8},{10,11... | collective-permute-start | bytes 860168 | tf_op jit(solution)/shard_map/ppermute | solution.py:324
  145.0 13.2 %collective-permute-start.27 = (bf16[16,8960]{1,0:T(8,128)(2,1)S(1)}, bf16[16,8960]{1,0:T(8,128)(2,1)S(1)}, u32[]{:S(2)}, u32[]{:S(2)}) collective-permute-start(bf16[16,8960]{1,0:T(8,128)(2,1)S(1)} %collective-permute-done.19.refs_4_), channel_id=1, source_target_pairs={{0,1},{1,0},{2,3},{3,2},{4,5},{5,4},{6,7},{7,6},{8,9},{9,8},{10,11... | collective-permute-start | bytes 860168 | tf_op jit(solution)/shard_map/ppermute | solution.py:324
  146.5 17.8 %collective-permute-start.28 = (bf16[16,8960]{1,0:T(8,128)(2,1)S(1)}, bf16[16,8960]{1,0:T(8,128)(2,1)S(1)}, u32[]{:S(2)}, u32[]{:S(2)}) collective-permute-start(bf16[16,8960]{1,0:T(8,128)(2,1)S(1)} %collective-permute-done.20.refs_5_), channel_id=1, source_target_pairs={{0,1},{1,0},{2,3},{3,2},{4,5},{5,4},{6,7},{7,6},{8,9},{9,8},{10,11... | collective-permute-start | bytes 860168 | tf_op jit(solution)/shard_map/ppermute | solution.py:324
  146.5 23.8 %collective-permute-start.29 = (bf16[16,8960]{1,0:T(8,128)(2,1)S(1)}, bf16[16,8960]{1,0:T(8,128)(2,1)S(1)}, u32[]{:S(2)}, u32[]{:S(2)}) collective-permute-start(bf16[16,8960]{1,0:T(8,128)(2,1)S(1)} %collective-permute-done.21.refs_6_), channel_id=1, source_target_pairs={{0,1},{1,0},{2,3},{3,2},{4,5},{5,4},{6,7},{7,6},{8,9},{9,8},{10,11... | collective-permute-start | bytes 860168 | tf_op jit(solution)/shard_map/ppermute | solution.py:324
  148.0 27.6 %collective-permute-start.30 = (bf16[16,8960]{1,0:T(8,128)(2,1)S(1)}, bf16[16,8960]{1,0:T(8,128)(2,1)S(1)}, u32[]{:S(2)}, u32[]{:S(2)}) collective-permute-start(bf16[16,8960]{1,0:T(8,128)(2,1)S(1)} %collective-permute-done.22.refs_7_), channel_id=1, source_target_pairs={{0,1},{1,0},{2,3},{3,2},{4,5},{5,4},{6,7},{7,6},{8,9},{9,8},{10,11... | collective-permute-start | bytes 860168 | tf_op jit(solution)/shard_map/ppermute | solution.py:324
  152.0 33.9 %collective-permute-start.6 = (bf16[16,8960]{1,0:T(8,128)(2,1)S(1)}, bf16[16,8960]{1,0:T(8,128)(2,1)}, u32[]{:S(2)}, u32[]{:S(2)}) collective-permute-start(bf16[16,8960]{1,0:T(8,128)(2,1)S(1)} %get-tuple-element.89), channel_id=1, source_target_pairs={{0,26},{2,28},{4,30},{6,0},{8,2},{10,4},{12,6},{14,8},{16,10},{18,... | collective-permute-start | bytes 860168 | tf_op jit(solution)/shard_map/ppermute | solution.py:328
  158.2 28.0 %collective-permute-start.7 = (bf16[16,8960]{1,0:T(8,128)(2,1)S(1)}, bf16[16,8960]{1,0:T(8,128)(2,1)}, u32[]{:S(2)}, u32[]{:S(2)}) collective-permute-start(bf16[16,8960]{1,0:T(8,128)(2,1)S(1)} %get-tuple-element.90), channel_id=1, source_target_pairs={{0,30},{2,0},{4,2},{6,4},{8,6},{10,8},{12,10},{14,12},{16,14},{18,... | collective-permute-start | bytes 860168 | tf_op jit(solution)/shard_map/ppermute | solution.py:328
  164.2 23.2 %collective-permute-start = (bf16[16,8960]{1,0:T(8,128)(2,1)S(1)}, bf16[16,8960]{1,0:T(8,128)(2,1)}, u32[]{:S(2)}, u32[]{:S(2)}) collective-permute-start(bf16[16,8960]{1,0:T(8,128)(2,1)S(1)} %get-tuple-element.83), channel_id=1, source_target_pairs={{0,2},{2,4},{4,6},{6,8},{8,10},{10,12},{12,14},{14,16},{16,18},{18... | collective-permute-start | bytes 860168 | tf_op jit(solution)/shard_map/ppermute | solution.py:328
  170.4 17.3 %collective-permute-start.1 = (bf16[16,8960]{1,0:T(8,128)(2,1)S(1)}, bf16[16,8960]{1,0:T(8,128)(2,1)}, u32[]{:S(2)}, u32[]{:S(2)}) collective-permute-start(bf16[16,8960]{1,0:T(8,128)(2,1)S(1)} %get-tuple-element.84), channel_id=1, source_target_pairs={{0,6},{2,8},{4,10},{6,12},{8,14},{10,16},{12,18},{14,20},{16,22},{... | collective-permute-start | bytes 860168 | tf_op jit(solution)/shard_map/ppermute | solution.py:328
  175.6 13.3 %collective-permute-start.10 = (bf16[16,8960]{1,0:T(8,128)(2,1)S(1)}, bf16[16,8960]{1,0:T(8,128)(2,1)S(1)}, u32[]{:S(2)}, u32[]{:S(2)}) collective-permute-start(bf16[16,8960]{1,0:T(8,128)(2,1)S(1)} %collective-permute-done.2.refs_2_), channel_id=1, source_target_pairs={{0,1},{1,0},{2,3},{3,2},{4,5},{5,4},{6,7},{7,6},{8,9},{9,8},{10,11... | collective-permute-start | bytes 860168 | tf_op jit(solution)/shard_map/ppermute | solution.py:324
  185.9 23.2 %collective-permute-start.31 = (bf16[320,512]{1,0:T(8,128)(2,1)S(1)}, bf16[320,512]{1,0:T(8,128)(2,1)S(1)}, u32[]{:S(2)}, u32[]{:S(2)}) collective-permute-start(bf16[320,512]{1,0:T(8,128)(2,1)S(1)} %inward.2.refs_0_), channel_id=1, source_target_pairs={{0,1},{1,0},{2,3},{3,2},{4,5},{5,4},{6,7},{7,6},{8,9},{9,8},{10,11... | collective-permute-start | bytes 983048 | tf_op jit(solution)/shard_map/ppermute | solution.py:324
  186.2 15.6 %collective-permute-start.11 = (bf16[16,8960]{1,0:T(8,128)(2,1)S(1)}, bf16[16,8960]{1,0:T(8,128)(2,1)S(1)}, u32[]{:S(2)}, u32[]{:S(2)}) collective-permute-start(bf16[16,8960]{1,0:T(8,128)(2,1)S(1)} %collective-permute-done.3.refs_3_), channel_id=1, source_target_pairs={{0,1},{1,0},{2,3},{3,2},{4,5},{5,4},{6,7},{7,6},{8,9},{9,8},{10,11... | collective-permute-start | bytes 860168 | tf_op jit(solution)/shard_map/ppermute | solution.py:324
  187.4 20.6 %collective-permute-start.12 = (bf16[16,8960]{1,0:T(8,128)(2,1)S(1)}, bf16[16,8960]{1,0:T(8,128)(2,1)S(1)}, u32[]{:S(2)}, u32[]{:S(2)}) collective-permute-start(bf16[16,8960]{1,0:T(8,128)(2,1)S(1)} %collective-permute-done.4.refs_4_), channel_id=1, source_target_pairs={{0,1},{1,0},{2,3},{3,2},{4,5},{5,4},{6,7},{7,6},{8,9},{9,8},{10,11... | collective-permute-start | bytes 860168 | tf_op jit(solution)/shard_map/ppermute | solution.py:324
  187.7 29.7 %collective-permute-start.13 = (bf16[16,8960]{1,0:T(8,128)(2,1)}, bf16[16,8960]{1,0:T(8,128)(2,1)}, u32[]{:S(2)}, u32[]{:S(2)}) collective-permute-start(bf16[16,8960]{1,0:T(8,128)(2,1)} %collective-permute-done.5.refs_5_), channel_id=1, source_target_pairs={{0,1},{1,0},{2,3},{3,2},{4,5},{5,4},{6,7},{7,6},{8,9},{9,8},{10,11... | collective-permute-start | bytes 860168 | tf_op jit(solution)/shard_map/ppermute | solution.py:324
  189.6 30.8 %collective-permute-start.14 = (bf16[16,8960]{1,0:T(8,128)(2,1)}, bf16[16,8960]{1,0:T(8,128)(2,1)}, u32[]{:S(2)}, u32[]{:S(2)}) collective-permute-start(bf16[16,8960]{1,0:T(8,128)(2,1)} %collective-permute-done.6.refs_6_), channel_id=1, source_target_pairs={{0,1},{1,0},{2,3},{3,2},{4,5},{5,4},{6,7},{7,6},{8,9},{9,8},{10,11... | collective-permute-start | bytes 860168 | tf_op jit(solution)/shard_map/ppermute | solution.py:324
  202.5 24.0 %collective-permute-start.15 = (bf16[16,8960]{1,0:T(8,128)(2,1)}, bf16[16,8960]{1,0:T(8,128)(2,1)}, u32[]{:S(2)}, u32[]{:S(2)}) collective-permute-start(bf16[16,8960]{1,0:T(8,128)(2,1)} %collective-permute-done.7.refs_7_), channel_id=1, source_target_pairs={{0,1},{1,0},{2,3},{3,2},{4,5},{5,4},{6,7},{7,6},{8,9},{9,8},{10,11... | collective-permute-start | bytes 860168 | tf_op jit(solution)/shard_map/ppermute | solution.py:324
  208.8 23.8 %collective-permute-start.8 = (bf16[16,8960]{1,0:T(8,128)(2,1)}, bf16[16,8960]{1,0:T(8,128)(2,1)}, u32[]{:S(2)}, u32[]{:S(2)}) collective-permute-start(bf16[16,8960]{1,0:T(8,128)(2,1)} %collective-permute-done.refs_0_), channel_id=1, source_target_pairs={{0,1},{1,0},{2,3},{3,2},{4,5},{5,4},{6,7},{7,6},{8,9},{9,8},{10,11... | collective-permute-start | bytes 860168 | tf_op jit(solution)/shard_map/ppermute | solution.py:324
  209.1 29.6 %collective-permute-start.9 = (bf16[16,8960]{1,0:T(8,128)(2,1)}, bf16[16,8960]{1,0:T(8,128)(2,1)}, u32[]{:S(2)}, u32[]{:S(2)}) collective-permute-start(bf16[16,8960]{1,0:T(8,128)(2,1)} %collective-permute-done.1.refs_1_), channel_id=1, source_target_pairs={{0,1},{1,0},{2,3},{3,2},{4,5},{5,4},{6,7},{7,6},{8,9},{9,8},{10,11... | collective-permute-start | bytes 860168 | tf_op jit(solution)/shard_map/ppermute | solution.py:324
  217.4 23.3 %collective-permute-start.32 = (bf16[16,4480]{1,0:T(8,128)(2,1)S(1)}, bf16[16,4480]{1,0:T(8,128)(2,1)S(1)}, u32[]{:S(2)}, u32[]{:S(2)}) collective-permute-start(bf16[16,4480]{1,0:T(8,128)(2,1)S(1)} %get-tuple-element.100), channel_id=1, source_target_pairs={{0,28},{1,29},{2,30},{3,31},{4,0},{5,1},{6,2},{7,3},{8,4},{9,5},{1... | collective-permute-start | bytes 430088 | tf_op jit(solution)/shard_map/ppermute | solution.py:336
  220.4 20.4 %collective-permute-start.33 = (bf16[16,4480]{1,0:T(8,128)(2,1)S(1)}, bf16[16,4480]{1,0:T(8,128)(2,1)S(1)}, u32[]{:S(2)}, u32[]{:S(2)}) collective-permute-start(bf16[16,4480]{1,0:T(8,128)(2,1)S(1)} %get-tuple-element.101), channel_id=1, source_target_pairs={{0,24},{1,25},{2,26},{3,27},{4,28},{5,29},{6,30},{7,31},{8,0},{9,1... | collective-permute-start | bytes 430088 | tf_op jit(solution)/shard_map/ppermute | solution.py:336
  226.5 14.5 %collective-permute-start.34 = (bf16[16,4480]{1,0:T(8,128)(2,1)S(1)}, bf16[16,4480]{1,0:T(8,128)(2,1)S(1)}, u32[]{:S(2)}, u32[]{:S(2)}) collective-permute-start(bf16[16,4480]{1,0:T(8,128)(2,1)S(1)} %get-tuple-element.102), channel_id=1, source_target_pairs={{0,20},{1,21},{2,22},{3,23},{4,24},{5,25},{6,26},{7,27},{8,28},{9,... | collective-permute-start | bytes 430088 | tf_op jit(solution)/shard_map/ppermute | solution.py:336
  232.7 11.0 %collective-permute-start.35 = (bf16[16,4480]{1,0:T(8,128)(2,1)S(1)}, bf16[16,4480]{1,0:T(8,128)(2,1)S(1)}, u32[]{:S(2)}, u32[]{:S(2)}) collective-permute-start(bf16[16,4480]{1,0:T(8,128)(2,1)S(1)} %get-tuple-element.103), channel_id=1, source_target_pairs={{0,16},{1,17},{2,18},{3,19},{4,20},{5,21},{6,22},{7,23},{8,24},{9,... | collective-permute-start | bytes 430088 | tf_op jit(solution)/shard_map/ppermute | solution.py:336
  238.7 8.0 %collective-permute-start.36 = (bf16[16,4480]{1,0:T(8,128)(2,1)S(1)}, bf16[16,4480]{1,0:T(8,128)(2,1)S(1)}, u32[]{:S(2)}, u32[]{:S(2)}) collective-permute-start(bf16[16,4480]{1,0:T(8,128)(2,1)S(1)} %get-tuple-element.104), channel_id=1, source_target_pairs={{0,12},{1,13},{2,14},{3,15},{4,16},{5,17},{6,18},{7,19},{8,20},{9,... | collective-permute-start | bytes 430088 | tf_op jit(solution)/shard_map/ppermute | solution.py:336
  240.8 9.0 %collective-permute-start.37 = (bf16[16,4480]{1,0:T(8,128)(2,1)S(1)}, bf16[16,4480]{1,0:T(8,128)(2,1)S(1)}, u32[]{:S(2)}, u32[]{:S(2)}) collective-permute-start(bf16[16,4480]{1,0:T(8,128)(2,1)S(1)} %get-tuple-element.105), channel_id=1, source_target_pairs={{0,8},{1,9},{2,10},{3,11},{4,12},{5,13},{6,14},{7,15},{8,16},{9,17... | collective-permute-start | bytes 430088 | tf_op jit(solution)/shard_map/ppermute | solution.py:336
  240.8 12.1 %collective-permute-start.38 = (bf16[16,4480]{1,0:T(8,128)(2,1)S(1)}, bf16[16,4480]{1,0:T(8,128)(2,1)S(1)}, u32[]{:S(2)}, u32[]{:S(2)}) collective-permute-start(bf16[16,4480]{1,0:T(8,128)(2,1)S(1)} %get-tuple-element.106), channel_id=1, source_target_pairs={{0,4},{1,5},{2,6},{3,7},{4,8},{5,9},{6,10},{7,11},{8,12},{9,13},{1... | collective-permute-start | bytes 430088 | tf_op jit(solution)/shard_map/ppermute | solution.py:336
  262.8 11.5 %collective-permute-start.47 = (bf16[320,512]{1,0:T(8,128)(2,1)S(1)}, bf16[320,512]{1,0:T(8,128)(2,1)S(1)}, u32[]{:S(2)}, u32[]{:S(2)}) collective-permute-start(bf16[320,512]{1,0:T(8,128)(2,1)S(1)} %inward.3.refs_0_), channel_id=1, source_target_pairs={{0,1},{1,0},{2,3},{3,2},{4,5},{5,4},{6,7},{7,6},{8,9},{9,8},{10,11... | collective-permute-start | bytes 983048 | tf_op jit(solution)/shard_map/ppermute | solution.py:324
  262.9 18.7 %collective-permute-start.39 = (bf16[16,4480]{1,0:T(8,128)(2,1)S(1)}, bf16[16,4480]{1,0:T(8,128)(2,1)S(1)}, u32[]{:S(2)}, u32[]{:S(2)}) collective-permute-start(bf16[16,4480]{1,0:T(8,128)(2,1)S(1)} %get-tuple-element.115), channel_id=1, source_target_pairs={{0,1},{1,0},{2,3},{3,2},{4,5},{5,4},{6,7},{7,6},{8,9},{9,8},{10,11... | collective-permute-start | bytes 430088 | tf_op jit(solution)/shard_map/ppermute | solution.py:336
  264.3 20.3 %collective-permute-start.40 = (bf16[16,4480]{1,0:T(8,128)(2,1)S(1)}, bf16[16,4480]{1,0:T(8,128)(2,1)S(1)}, u32[]{:S(2)}, u32[]{:S(2)}) collective-permute-start(bf16[16,4480]{1,0:T(8,128)(2,1)S(1)} %get-tuple-element.116), channel_id=1, source_target_pairs={{0,29},{1,28},{2,31},{3,30},{4,1},{5,0},{6,3},{7,2},{8,5},{9,4},{1... | collective-permute-start | bytes 430088 | tf_op jit(solution)/shard_map/ppermute | solution.py:336
  270.1 17.6 %collective-permute-start.41 = (bf16[16,4480]{1,0:T(8,128)(2,1)S(1)}, bf16[16,4480]{1,0:T(8,128)(2,1)S(1)}, u32[]{:S(2)}, u32[]{:S(2)}) collective-permute-start(bf16[16,4480]{1,0:T(8,128)(2,1)S(1)} %get-tuple-element.117), channel_id=1, source_target_pairs={{0,25},{1,24},{2,27},{3,26},{4,29},{5,28},{6,31},{7,30},{8,1},{9,0... | collective-permute-start | bytes 430088 | tf_op jit(solution)/shard_map/ppermute | solution.py:336
  271.3 16.6 %collective-permute-start.42 = (bf16[16,4480]{1,0:T(8,128)(2,1)S(1)}, bf16[16,4480]{1,0:T(8,128)(2,1)S(1)}, u32[]{:S(2)}, u32[]{:S(2)}) collective-permute-start(bf16[16,4480]{1,0:T(8,128)(2,1)S(1)} %get-tuple-element.118), channel_id=1, source_target_pairs={{0,21},{1,20},{2,23},{3,22},{4,25},{5,24},{6,27},{7,26},{8,29},{9,... | collective-permute-start | bytes 430088 | tf_op jit(solution)/shard_map/ppermute | solution.py:336
  274.3 25.0 %collective-permute-start.43 = (bf16[16,4480]{1,0:T(8,128)(2,1)S(1)}, bf16[16,4480]{1,0:T(8,128)(2,1)S(1)}, u32[]{:S(2)}, u32[]{:S(2)}) collective-permute-start(bf16[16,4480]{1,0:T(8,128)(2,1)S(1)} %get-tuple-element.119), channel_id=1, source_target_pairs={{0,17},{1,16},{2,19},{3,18},{4,21},{5,20},{6,23},{7,22},{8,25},{9,... | collective-permute-start | bytes 430088 | tf_op jit(solution)/shard_map/ppermute | solution.py:336
  281.6 20.3 %collective-permute-start.44 = (bf16[16,4480]{1,0:T(8,128)(2,1)S(1)}, bf16[16,4480]{1,0:T(8,128)(2,1)S(1)}, u32[]{:S(2)}, u32[]{:S(2)}) collective-permute-start(bf16[16,4480]{1,0:T(8,128)(2,1)S(1)} %get-tuple-element.120), channel_id=1, source_target_pairs={{0,13},{1,12},{2,15},{3,14},{4,17},{5,16},{6,19},{7,18},{8,21},{9,... | collective-permute-start | bytes 430088 | tf_op jit(solution)/shard_map/ppermute | solution.py:336
  284.6 17.2 %collective-permute-start.45 = (bf16[16,4480]{1,0:T(8,128)(2,1)S(1)}, bf16[16,4480]{1,0:T(8,128)(2,1)S(1)}, u32[]{:S(2)}, u32[]{:S(2)}) collective-permute-start(bf16[16,4480]{1,0:T(8,128)(2,1)S(1)} %get-tuple-element.121), channel_id=1, source_target_pairs={{0,9},{1,8},{2,11},{3,10},{4,13},{5,12},{6,15},{7,14},{8,17},{9,16... | collective-permute-start | bytes 430088 | tf_op jit(solution)/shard_map/ppermute | solution.py:336
  287.7 20.2 %collective-permute-start.46 = (bf16[16,4480]{1,0:T(8,128)(2,1)S(1)}, bf16[16,4480]{1,0:T(8,128)(2,1)S(1)}, u32[]{:S(2)}, u32[]{:S(2)}) collective-permute-start(bf16[16,4480]{1,0:T(8,128)(2,1)S(1)} %get-tuple-element.122), channel_id=1, source_target_pairs={{0,5},{1,4},{2,7},{3,6},{4,9},{5,8},{6,11},{7,10},{8,13},{9,12},{1... | collective-permute-start | bytes 430088 | tf_op jit(solution)/shard_map/ppermute | solution.py:336
  287.9 21.1 %collective-permute-start.48 = (bf16[16,4480]{1,0:T(8,128)(2,1)S(1)}, bf16[16,4480]{1,0:T(8,128)(2,1)S(1)}, u32[]{:S(2)}, u32[]{:S(2)}) collective-permute-start(bf16[16,4480]{1,0:T(8,128)(2,1)S(1)} %get-tuple-element.139), channel_id=1, source_target_pairs={{0,30},{1,31},{2,0},{3,1},{4,2},{5,3},{6,4},{7,5},{8,6},{9,7},{10,... | collective-permute-start | bytes 430088 | tf_op jit(solution)/shard_map/ppermute | solution.py:336
  299.3 11.3 %collective-permute-start.49 = (bf16[16,4480]{1,0:T(8,128)(2,1)S(1)}, bf16[16,4480]{1,0:T(8,128)(2,1)S(1)}, u32[]{:S(2)}, u32[]{:S(2)}) collective-permute-start(bf16[16,4480]{1,0:T(8,128)(2,1)S(1)} %get-tuple-element.140), channel_id=1, source_target_pairs={{0,26},{1,27},{2,28},{3,29},{4,30},{5,31},{6,0},{7,1},{8,2},{9,3},... | collective-permute-start | bytes 430088 | tf_op jit(solution)/shard_map/ppermute | solution.py:336
  301.8 16.9 %collective-permute-start.50 = (bf16[16,4480]{1,0:T(8,128)(2,1)S(1)}, bf16[16,4480]{1,0:T(8,128)(2,1)S(1)}, u32[]{:S(2)}, u32[]{:S(2)}) collective-permute-start(bf16[16,4480]{1,0:T(8,128)(2,1)S(1)} %get-tuple-element.141), channel_id=1, source_target_pairs={{0,22},{1,23},{2,24},{3,25},{4,26},{5,27},{6,28},{7,29},{8,30},{9,... | collective-permute-start | bytes 430088 | tf_op jit(solution)/shard_map/ppermute | solution.py:336
  301.8 20.5 %collective-permute-start.51 = (bf16[16,4480]{1,0:T(8,128)(2,1)S(1)}, bf16[16,4480]{1,0:T(8,128)(2,1)S(1)}, u32[]{:S(2)}, u32[]{:S(2)}) collective-permute-start(bf16[16,4480]{1,0:T(8,128)(2,1)S(1)} %get-tuple-element.142), channel_id=1, source_target_pairs={{0,18},{1,19},{2,20},{3,21},{4,22},{5,23},{6,24},{7,25},{8,26},{9,... | collective-permute-start | bytes 430088 | tf_op jit(solution)/shard_map/ppermute | solution.py:336
  307.9 21.1 %collective-permute-start.52 = (bf16[16,4480]{1,0:T(8,128)(2,1)S(1)}, bf16[16,4480]{1,0:T(8,128)(2,1)S(1)}, u32[]{:S(2)}, u32[]{:S(2)}) collective-permute-start(bf16[16,4480]{1,0:T(8,128)(2,1)S(1)} %get-tuple-element.143), channel_id=1, source_target_pairs={{0,14},{1,15},{2,16},{3,17},{4,18},{5,19},{6,20},{7,21},{8,22},{9,... | collective-permute-start | bytes 430088 | tf_op jit(solution)/shard_map/ppermute | solution.py:336
  308.9 21.5 %collective-permute-start.53 = (bf16[16,4480]{1,0:T(8,128)(2,1)S(1)}, bf16[16,4480]{1,0:T(8,128)(2,1)S(1)}, u32[]{:S(2)}, u32[]{:S(2)}) collective-permute-start(bf16[16,4480]{1,0:T(8,128)(2,1)S(1)} %get-tuple-element.144), channel_id=1, source_target_pairs={{0,10},{1,11},{2,12},{3,13},{4,14},{5,15},{6,16},{7,17},{8,18},{9,... | collective-permute-start | bytes 430088 | tf_op jit(solution)/shard_map/ppermute | solution.py:336
  310.6 23.0 %collective-permute-start.54 = (bf16[16,4480]{1,0:T(8,128)(2,1)S(1)}, bf16[16,4480]{1,0:T(8,128)(2,1)S(1)}, u32[]{:S(2)}, u32[]{:S(2)}) collective-permute-start(bf16[16,4480]{1,0:T(8,128)(2,1)S(1)} %get-tuple-element.145), channel_id=1, source_target_pairs={{0,6},{1,7},{2,8},{3,9},{4,10},{5,11},{6,12},{7,13},{8,14},{9,15},... | collective-permute-start | bytes 430088 | tf_op jit(solution)/shard_map/ppermute | solution.py:336
  318.7 16.2 %collective-permute-start.55 = (bf16[16,4480]{1,0:T(8,128)(2,1)S(1)}, bf16[16,4480]{1,0:T(8,128)(2,1)S(1)}, u32[]{:S(2)}, u32[]{:S(2)}) collective-permute-start(bf16[16,4480]{1,0:T(8,128)(2,1)S(1)} %get-tuple-element.146), channel_id=1, source_target_pairs={{0,2},{1,3},{2,4},{3,5},{4,6},{5,7},{6,8},{7,9},{8,10},{9,11},{10,... | collective-permute-start | bytes 430088 | tf_op jit(solution)/shard_map/ppermute | solution.py:336
  322.4 14.7 %collective-permute-start.56 = (bf16[16,4480]{1,0:T(8,128)(2,1)S(1)}, bf16[16,4480]{1,0:T(8,128)(2,1)S(1)}, u32[]{:S(2)}, u32[]{:S(2)}) collective-permute-start(bf16[16,4480]{1,0:T(8,128)(2,1)S(1)} %get-tuple-element.147), channel_id=1, source_target_pairs={{0,31},{1,30},{2,1},{3,0},{4,3},{5,2},{6,5},{7,4},{8,7},{9,6},{10,... | collective-permute-start | bytes 430088 | tf_op jit(solution)/shard_map/ppermute | solution.py:336
  329.0 11.2 %collective-permute-start.57 = (bf16[16,4480]{1,0:T(8,128)(2,1)S(1)}, bf16[16,4480]{1,0:T(8,128)(2,1)S(1)}, u32[]{:S(2)}, u32[]{:S(2)}) collective-permute-start(bf16[16,4480]{1,0:T(8,128)(2,1)S(1)} %get-tuple-element.148), channel_id=1, source_target_pairs={{0,27},{1,26},{2,29},{3,28},{4,31},{5,30},{6,1},{7,0},{8,3},{9,2},... | collective-permute-start | bytes 430088 | tf_op jit(solution)/shard_map/ppermute | solution.py:336
  330.5 12.5 %collective-permute-start.58 = (bf16[16,4480]{1,0:T(8,128)(2,1)S(1)}, bf16[16,4480]{1,0:T(8,128)(2,1)S(1)}, u32[]{:S(2)}, u32[]{:S(2)}) collective-permute-start(bf16[16,4480]{1,0:T(8,128)(2,1)S(1)} %get-tuple-element.149), channel_id=1, source_target_pairs={{0,23},{1,22},{2,25},{3,24},{4,27},{5,26},{6,29},{7,28},{8,31},{9,... | collective-permute-start | bytes 430088 | tf_op jit(solution)/shard_map/ppermute | solution.py:336
  333.5 23.8 %collective-permute-start.59 = (bf16[16,4480]{1,0:T(8,128)(2,1)S(1)}, bf16[16,4480]{1,0:T(8,128)(2,1)S(1)}, u32[]{:S(2)}, u32[]{:S(2)}) collective-permute-start(bf16[16,4480]{1,0:T(8,128)(2,1)S(1)} %get-tuple-element.150), channel_id=1, source_target_pairs={{0,19},{1,18},{2,21},{3,20},{4,23},{5,22},{6,25},{7,24},{8,27},{9,... | collective-permute-start | bytes 430088 | tf_op jit(solution)/shard_map/ppermute | solution.py:336
  334.9 22.5 %collective-permute-start.60 = (bf16[16,4480]{1,0:T(8,128)(2,1)S(1)}, bf16[16,4480]{1,0:T(8,128)(2,1)S(1)}, u32[]{:S(2)}, u32[]{:S(2)}) collective-permute-start(bf16[16,4480]{1,0:T(8,128)(2,1)S(1)} %get-tuple-element.151), channel_id=1, source_target_pairs={{0,15},{1,14},{2,17},{3,16},{4,19},{5,18},{6,21},{7,20},{8,23},{9,... | collective-permute-start | bytes 430088 | tf_op jit(solution)/shard_map/ppermute | solution.py:336
  337.1 20.3 %collective-permute-start.61 = (bf16[16,4480]{1,0:T(8,128)(2,1)S(1)}, bf16[16,4480]{1,0:T(8,128)(2,1)S(1)}, u32[]{:S(2)}, u32[]{:S(2)}) collective-permute-start(bf16[16,4480]{1,0:T(8,128)(2,1)S(1)} %get-tuple-element.152), channel_id=1, source_target_pairs={{0,11},{1,10},{2,13},{3,12},{4,15},{5,14},{6,17},{7,16},{8,19},{9,... | collective-permute-start | bytes 430088 | tf_op jit(solution)/shard_map/ppermute | solution.py:336
  340.3 18.3 %collective-permute-start.62 = (bf16[16,4480]{1,0:T(8,128)(2,1)S(1)}, bf16[16,4480]{1,0:T(8,128)(2,1)S(1)}, u32[]{:S(2)}, u32[]{:S(2)}) collective-permute-start(bf16[16,4480]{1,0:T(8,128)(2,1)S(1)} %get-tuple-element.153), channel_id=1, source_target_pairs={{0,7},{1,6},{2,9},{3,8},{4,11},{5,10},{6,13},{7,12},{8,15},{9,14},... | collective-permute-start | bytes 430088 | tf_op jit(solution)/shard_map/ppermute | solution.py:336
  342.9 18.7 %collective-permute-start.63 = (bf16[16,4480]{1,0:T(8,128)(2,1)S(1)}, bf16[16,4480]{1,0:T(8,128)(2,1)S(1)}, u32[]{:S(2)}, u32[]{:S(2)}) collective-permute-start(bf16[16,4480]{1,0:T(8,128)(2,1)S(1)} %get-tuple-element.154), channel_id=1, source_target_pairs={{0,3},{1,2},{2,5},{3,4},{4,7},{5,6},{6,9},{7,8},{8,11},{9,10},{10,... | collective-permute-start | bytes 430088 | tf_op jit(solution)/shard_map/ppermute | solution.py:336
  (13 other events, 293.6 us)

commit v2 on v0

v2 whole, which is shorter than its diff:
```python
import functools

import jax
import jax.numpy as jnp
from jax import lax
from jax.experimental import pallas as pl
from jax.experimental.pallas import tpu as pltpu
from jax.sharding import PartitionSpec as P

FOLDS = (1, 1, 2)
STEPS = 4
VMEM = 58 * 1024 * 1024
F32 = jnp.float32
BF16 = jnp.bfloat16


def dot(a, b):
    return lax.dot_general(a, b, (((1,), (0,)), ((), ())), preferred_element_type=F32)


def dot_nt(a, b):
    return lax.dot_general(a, b, (((1,), (1,)), ((), ())), preferred_element_type=F32)


def as_mask(cond):
    return jnp.where(cond, 1.0, 0.0).astype(BF16)


def placed(aux_ref, group, rows, shift):
    row = lax.broadcasted_iota(jnp.int32, (rows, aux_ref.shape[1]), 0).astype(F32) - shift
    at = 2 + 2 * group
    return [row == aux_ref[at + k : at + k + 1, :] for k in range(2)]


def pack_group(base, group, aux_ref, normed, pack_ref):
    fold = FOLDS[group]
    cols = pack_ref.shape[1]
    block = min(cols, normed.shape[1] // STEPS)
    picks = []
    for h in range(fold):
        first, second = placed(aux_ref, group, pack_ref.shape[0], h * (base // fold))
        picks.append(as_mask(first | second))
    for c in range(0, cols, block):
        total = None
        for h in range(fold):
            term = dot(picks[h], normed[:, h * cols + c : h * cols + c + block])
            total = term if total is None else total + term
        pack_ref[:, c : c + block] = total.astype(BF16)


def first_kernel(base, attn_ref, res_ref, gain_ref, router_ref, ids_ref, aux_ref, normed_ref, pack_ref, held):
    tokens, width = res_ref.shape
    experts = router_ref.shape[0]
    quarter = width // STEPS
    total = jnp.zeros((tokens, 1), F32)
    for k in range(STEPS):
        cols = slice(k * quarter, (k + 1) * quarter)
        part = res_ref[:, cols].astype(F32) + attn_ref[cols, :].astype(F32).T
        held[:, cols] = part
        total += jnp.sum(part * part, axis=1, keepdims=True)
    scale = lax.rsqrt(total / width + 1e-06)
    logits = jnp.zeros((experts, tokens), F32)
    for k in range(STEPS):
        cols = slice(k * quarter, (k + 1) * quarter)
        piece = (held[:, cols] * scale * gain_ref[:, cols].astype(F32)).astype(BF16)
        normed_ref[:, cols] = piece
        logits += dot_nt(router_ref[:, cols], piece)
    affinity = jax.nn.sigmoid(logits)
    expert = lax.broadcasted_iota(jnp.int32, (experts, tokens), 0)
    hit = [expert == ids_ref[k : k + 1, :] for k in range(2)]
    named = as_mask(hit[0] | hit[1])
    first = lax.broadcasted_iota(jnp.int32, (tokens, tokens), 0)
    second = lax.broadcasted_iota(jnp.int32, (tokens, tokens), 1)
    before = dot(named, as_mask(first < second))
    chosen = [jnp.sum(jnp.where(h, affinity, 0.0), axis=0, keepdims=True) for h in hit]
    ranks = [
        jnp.sum(jnp.where(h, before, 0.0), axis=0, keepdims=True).astype(jnp.int32) for h in hit
    ]
    denom = chosen[0] + chosen[1]
    for k in range(2):
        aux_ref[k : k + 1, :] = 2.5 * chosen[k] / denom
        start = 0
        for g, fold in enumerate(FOLDS):
            slots = base // fold
            inside = (ranks[k] >= start) & (ranks[k] < start + slots)
            row = ids_ref[k : k + 1, :] * base + ranks[k] - start
            at = 2 + 2 * g + k
            aux_ref[at : at + 1, :] = jnp.where(inside, row, -experts * base).astype(F32)
            start += slots
    pack_group(base, 0, aux_ref, normed_ref, pack_ref)


def first(base, attn, residual, gain, router, ids):
    tokens, width = residual.shape
    rows = router.shape[0] * base
    return pl.pallas_call(
        functools.partial(first_kernel, base),
        out_shape=[
            jax.ShapeDtypeStruct((8, tokens), F32),
            jax.ShapeDtypeStruct((tokens, width), BF16),
            jax.ShapeDtypeStruct((rows, width // FOLDS[0]), BF16),
        ],
        scratch_shapes=[pltpu.VMEM((tokens, width), F32)],
        compiler_params=pltpu.CompilerParams(vmem_limit_bytes=VMEM),
        cost_estimate=pl.CostEstimate(
            flops=2 * rows * tokens * width, bytes_accessed=10 * tokens * width, transcendentals=0
        ),
        name="first",
    )(attn, residual, gain, router, ids)


def others_kernel(base, attn_ref, res_ref, aux_ref, normed_ref, stream_ref, *packs):
    for g, pack_ref in enumerate(packs):
        pack_group(base, g + 1, aux_ref, normed_ref, pack_ref)
    width = res_ref.shape[1]
    quarter = width // STEPS
    for k in range(STEPS):
        cols = slice(k * quarter, (k + 1) * quarter)
        stream_ref[:, cols] = res_ref[:, cols].astype(F32) + attn_ref[cols, :].astype(F32).T


def others(base, attn, residual, aux, normed, rows):
    tokens, width = residual.shape
    return pl.pallas_call(
        functools.partial(others_kernel, base),
        out_shape=[jax.ShapeDtypeStruct((tokens, width), F32)]
        + [jax.ShapeDtypeStruct((rows, width // fold), BF16) for fold in FOLDS[1:]],
        compiler_params=pltpu.CompilerParams(vmem_limit_bytes=VMEM),
        cost_estimate=pl.CostEstimate(
            flops=4 * rows * tokens * width, bytes_accessed=14 * tokens * width, transcendentals=0
        ),
        name="others",
    )(attn, residual, aux, normed)


def inward_kernel(base, fold, parts, *refs):
    piece_refs = refs[:parts]
    gate_ref, up_ref, out_ref, acc = refs[parts:]
    few = base // fold
    ff = gate_ref.shape[2]
    step = pl.program_id(0)

    @pl.when(step == 0)
    def _():
        acc[...] = jnp.zeros_like(acc)

    pieces = [ref[...] for ref in piece_refs]
    if fold > 1:
        part = step // (STEPS // fold)
        rows = pieces[0].shape[0]
        out_row = lax.broadcasted_iota(jnp.int32, (rows // fold, rows), 0)
        in_row = lax.broadcasted_iota(jnp.int32, (rows // fold, rows), 1)
        select = as_mask(in_row == (out_row // few) * base + part * few + out_row % few)
        pieces = [dot(select, piece).astype(BF16) for piece in pieces]
    block = jnp.concatenate(pieces, axis=0)
    acc[:, :ff] += dot(block, gate_ref[0])
    acc[:, ff:] += dot(block, up_ref[0])

    @pl.when(step == STEPS - 1)
    def _():
        gated = acc[:, :ff]
        out_ref[...] = (gated / (1.0 + jnp.exp(-gated)) * acc[:, ff:]).astype(BF16)


def inward(base, fold, pieces, gate, up):
    width, ff = gate.shape[1:]
    quarter = width // STEPS
    total = sum(piece.shape[0] for piece in pieces) // fold
    return pl.pallas_call(
        functools.partial(inward_kernel, base, fold, len(pieces)),
        grid=(STEPS,),
        in_specs=[
            pl.BlockSpec((piece.shape[0], quarter), lambda i: (0, i % (STEPS // fold)))
            for piece in pieces
        ]
        + [pl.BlockSpec((1, quarter, ff), lambda i: (0, i, 0))] * 2,
        out_specs=pl.BlockSpec((total, ff), lambda i: (0, 0)),
        out_shape=jax.ShapeDtypeStruct((total, ff), BF16),
        scratch_shapes=[pltpu.VMEM((total, 2 * ff), F32)],
        compiler_params=pltpu.CompilerParams(vmem_limit_bytes=VMEM),
        cost_estimate=pl.CostEstimate(flops=total, bytes_accessed=total, transcendentals=0),
        name="inward",
    )(*pieces, gate, up)


def outward_kernel(base, fold, parts, here_ref, *refs):
    hidden, (down_ref, out_ref), scratch = refs[:parts], refs[parts : parts + 2], refs[parts + 2 :]
    here = here_ref[0]
    rows = out_ref.shape[1]
    few = base // fold
    count = rows // base * few
    ff = hidden[0].shape[1]
    made = None
    for o in range(parts):
        order = [(j - o) % parts for j in range(parts)]
        block = jnp.concatenate([hidden[o][i * count : (i + 1) * count, :] for i in order], axis=0)
        at = pl.multiple_of(lax.rem(here + parts - o, parts) * ff, ff)
        term = dot_nt(block, down_ref[0, :, pl.ds(at, ff)])
        made = term if made is None else made + term
    made = made.astype(BF16)
    pieces = [made[j * count : (j + 1) * count] for j in range(parts)]
    owners = [lax.rem(here + parts - j, parts) for j in range(parts)]
    if fold == 1:
        for owner, piece in zip(owners, pieces):
            out_ref[owner] = piece
        return
    (folded,) = scratch
    part, last = pl.program_id(1), pl.num_programs(1) - 1
    out_row = lax.broadcasted_iota(jnp.int32, (rows, count), 0)
    in_row = lax.broadcasted_iota(jnp.int32, (rows, count), 1)
    place = as_mask(out_row == (in_row // few) * base + part * few + in_row % few)

    @pl.when(part == 0)
    def _():
        folded[...] = jnp.zeros_like(folded)

    for j in range(parts):
        folded[j] += dot(place, pieces[j])

    @pl.when(part == last)
    def _():
        for j in range(parts):
            out_ref[owners[j]] = folded[j].astype(BF16)


def outward(base, fold, back_fold, here, hidden, down):
    parts = len(hidden)
    total, ff = hidden[0].shape
    rows = total // parts * fold
    cols = down.shape[1]
    steps = max(s for s in (1, 2, STEPS) if cols % (128 * s) == 0)
    step = cols // steps
    outer = steps // back_fold
    return pl.pallas_call(
        functools.partial(outward_kernel, base, fold, parts),
        grid_spec=pltpu.PrefetchScalarGridSpec(
            num_scalar_prefetch=1,
            grid=(outer, back_fold),
            in_specs=[pl.BlockSpec((total, ff), lambda i, h, here: (0, 0))] * parts
            + [pl.BlockSpec((1, step, parts * ff), lambda i, h, here: (0, h * outer + i, 0))],
            out_specs=pl.BlockSpec((parts, rows, step), lambda i, h, here: (0, 0, i)),
            scratch_shapes=[pltpu.VMEM((parts, rows, step), F32)] if fold > 1 else [],
        ),
        out_shape=jax.ShapeDtypeStruct((parts, rows, cols // back_fold), BF16),
        compiler_params=pltpu.CompilerParams(vmem_limit_bytes=VMEM),
        cost_estimate=pl.CostEstimate(flops=total, bytes_accessed=total, transcendentals=0),
        name="outward",
    )(here, *hidden, down)


def combine_kernel(base, fold, back_fold, group, aux_ref, stream_ref, back_ref, out_ref):
    rows, cols = back_ref.shape[1:]
    for h in range(back_fold):
        hits = placed(aux_ref, group, rows, h * (base // fold))
        both = sum(jnp.where(hits[k], aux_ref[k : k + 1, :], 0.0) for k in range(2)).T
        high = both.astype(BF16)
        low = (both - high.astype(F32)).astype(BF16)
        block = back_ref[0]
        cut = slice(h * cols, (h + 1) * cols)
        total = stream_ref[:, cut] + (dot(low, block) + dot(high, block))
        out_ref[:, cut] = total.astype(out_ref.dtype)


def combine(base, fold, back_fold, group, aux, stream, back):
    parts, rows, wide = back.shape
    tokens, width = stream.shape
    cols = width // parts
    last = group == len(FOLDS) - 1
    return pl.pallas_call(
        functools.partial(combine_kernel, base, fold, back_fold, group),
        grid=(parts,),
        in_specs=[
            pl.BlockSpec(aux.shape, lambda i: (0, 0)),
            pl.BlockSpec((tokens, cols), lambda i: (0, i)),
            pl.BlockSpec((1, rows, wide), lambda i: (i, 0, 0)),
        ],
        out_specs=pl.BlockSpec((tokens, cols), lambda i: (0, i)),
        out_shape=jax.ShapeDtypeStruct((tokens, width), BF16 if last else F32),
        compiler_params=pltpu.CompilerParams(vmem_limit_bytes=VMEM),
        cost_estimate=pl.CostEstimate(
            flops=4 * tokens * rows * width,
            bytes_accessed=8 * tokens * width + 2 * rows * wide * parts,
            transcendentals=0,
        ),
        name="combine",
    )(aux, stream, back)


def body(
    attn_cols, residual, norm_gain, router_weight, expert_ids, gate_weight, up_weight, down_weight
):
    groups = lax.axis_size("dp")
    parts = lax.axis_size("blk")
    tokens, width = residual.shape
    experts = router_weight.shape[1]
    fanout = expert_ids.shape[1]
    assert gate_weight.shape[0] == 1 and fanout == 2
    capacity = max(2, (5 * tokens * fanout + 4 * experts - 1) // (4 * experts))
    base = capacity * 2 // 5
    assert sum(base // fold for fold in FOLDS) == capacity
    rows = experts * base
    cols = down_weight.shape[1]
    here = lax.axis_index("blk").astype(jnp.int32).reshape(1)

    def shared(block):
        shifts = [[(i, (i + o) % parts) for i in range(parts)] for o in range(1, parts)]
        return [block] + [lax.ppermute(block, "blk", perm) for perm in shifts]

    def dispatch(pack):
        pack = pack.reshape(groups, base, -1)
        got = lax.all_to_all(pack, "dp", split_axis=0, concat_axis=0, tiled=True)
        return got.reshape(rows, -1)

    held = attn_cols.shape[1]
    send = attn_cols.T.reshape(held, groups, tokens).transpose(1, 0, 2)
    attn = lax.all_to_all(send, "dp", split_axis=0, concat_axis=0, tiled=True)
    attn = attn.reshape(width, tokens)
    aux, normed, pack = first(
        base, attn, residual, norm_gain.reshape(1, width), router_weight.T, expert_ids.T
    )
    stream, *packs = others(base, attn, residual, aux, normed, rows)
    def returned(made):
        made = made.reshape(parts * groups, base, -1)
        back = lax.all_to_all(made, ("blk", "dp"), split_axis=0, concat_axis=0, tiled=True)
        return back.reshape(parts, rows, -1)

    def gate_up(group, pieces):
        return inward(base, FOLDS[group], pieces, gate_weight, up_weight)

    back_folds = [fold if cols % (128 * fold) == 0 else 1 for fold in FOLDS]

    def down(group, hidden):
        return outward(base, FOLDS[group], back_folds[group], here, hidden, down_weight)

    tie = lax.optimization_barrier
    arrived_a, arrived_b = dispatch(pack), dispatch(packs[0])
    pieces_a, pieces_b = shared(arrived_a), shared(arrived_b)
    pieces_a, pieces_b[0] = tie((pieces_a, pieces_b[0]))
    hidden = gate_up(0, pieces_a)
    hidden, pack_c = tie((hidden, packs[1]))
    arrived_c = dispatch(pack_c)
    made = down(0, shared(hidden))
    made, pieces_b, arrived_c = tie((made, pieces_b, arrived_c))
    back_a = returned(made)
    hidden = shared(gate_up(1, pieces_b))
    hidden, arrived_c = tie((hidden, arrived_c))
    pieces_c = shared(arrived_c)
    made = down(1, hidden)
    made, pieces_c = tie((made, pieces_c))
    back_b = returned(made)
    back_c = returned(down(2, shared(gate_up(2, pieces_c))))
    for group, back in enumerate((back_a, back_b, back_c)):
        stream = combine(base, FOLDS[group], back_folds[group], group, aux, stream, back)
    return stream


def solution(mesh):
    return jax.shard_map(
        body,
        mesh=mesh,
        in_specs=(
            P("blk", "dp"),
            P(("blk", "dp"), None),
            P(),
            P(),
            P(("blk", "dp"), None),
            P("dp", None, "blk"),
            P("dp", None, "blk"),
            P("dp", "blk", None),
        ),
        out_specs=P(("blk", "dp"), None),
        check_vma=False,
    )
```

time: 758 us -> 348 us (0.46)
  waiting for transfers between devices: 447 us -> 216 us
  blocking collectives: 125 us -> 0 us
  local copies, waits for them, and re-layouts: 99.3 us -> 10.4 us
  Pallas kernels: 0 us -> 74 us
  matrix products: 44.7 us -> 0 us
  starting transfers between devices: 13.1 us -> 43.1 us
  other arithmetic: 13.6 us -> 0 us
  between operations: 13.3 us -> 0.07 us
    all_gather x3 -> x0, waiting for transfers between devices: 293 us -> none  [the longest x1 166 us: body(): lax.all_gather(down_weight, 'blk', axis=1, tiled=True)]
    all_to_all x1 -> x0, blocking collectives: 125 us -> none  [body(): lax.all_to_all(outgoing.reshape(groups, exp_local * capacity, width), 'dp...]
    pallas_call x0 -> x11, Pallas kernels: none -> 74 us  [the longest x3 27.5 us: inward(): pl.pallas_call(functools.partial(inward_kernel, base, fold, len(pieces)),...]
    ppermute x0 -> x6, waiting for transfers between devices: none -> 70.6 us  [shared(): return [block] + [lax.ppermute(block, 'blk', perm) for perm in shifts]]
    dot_general x4 -> x0, matrix products: 44.7 us -> none  [the longest x2 21.6 us: project_in(): jnp.einsum('secd,edf->secf', arrived, piece, preferred_element_type=jnp.f...]
    reshape x4 -> x1, local copies, waits for them, and re-layouts: 31.1 us -> 0.63 us  [body(): norm_gain.reshape(1, width)]
    all_to_all x2 -> x7, starting transfers between devices: 13.1 us -> 36.8 us  [the longest x3 15.2 us: returned(): lax.all_to_all(made, ('blk', 'dp'), split_axis=0, concat_axis=0, tiled=True)]
    gather x6 -> x0, local copies, waits for them, and re-layouts: 13.3 us -> none  [the longest x1 10.9 us: body(): picked = returned[slots].reshape(tok_rows, fanout, width)]
  transfers between devices with their start and end apart: 5 -> 13, of which waited for: 4 -> 9; matrix products, arithmetic and copies ran while one was open for 10% -> 0% of each run, Pallas kernels for 0% -> 18%
where the time goes in v2:
time: 348 us; the launch traced here: 344 us
  waiting for transfers between devices  216 us (62%)
  Pallas kernels  74 us (21%)
  starting transfers between devices  43.1 us (12%)
  local copies, waits for them, and re-layouts  10.4 us (3%)
    all_to_all x3, waiting for transfers between devices, dispatch(): got = lax.all_to_all(pack, 'dp', split_axis=0, concat_axis=0, tiled=True)  76.8 us
    ppermute x6, waiting for transfers between devices, shared(): return [block] + [lax.ppermute(block, 'blk', perm) for perm in shifts]  70.6 us
    all_to_all x1, waiting for transfers between devices, body(): attn = lax.all_to_all(send, 'dp', split_axis=0, concat_axis=0, tiled=True)  41.2 us
    all_to_all x3, waiting for transfers between devices, returned(): lax.all_to_all(made, ('blk', 'dp'), split_axis=0, concat_axis=0, tiled=True)  27.8 us
    pallas_call x3, Pallas kernels, inward(): pl.pallas_call(functools.partial(inward_kernel, base, fold, len(pieces)),...  27.5 us
    pallas_call x3, Pallas kernels, outward(): pl.pallas_call(functools.partial(outward_kernel, base, fold, parts), grid...  20.3 us
    all_to_all x3, starting transfers between devices, returned(): lax.all_to_all(made, ('blk', 'dp'), split_axis=0, concat_axis=0, tiled=True)  15.2 us
    all_to_all x3, starting transfers between devices, dispatch(): got = lax.all_to_all(pack, 'dp', split_axis=0, concat_axis=0, tiled=True)  14.9 us
  transfers between devices with their start and end apart: 13, of which 9 were waited for; matrix products, arithmetic and copies ran while one was open for 0% of the time, Pallas kernels for 18%

profile of v2, /device:TPU:11, one launch (start us, length us, event | category | flops | bytes accessed | tf_op | source)
XLA Modules:
  0.0 344.0 jit_solution(15964915880039691232)
XLA Ops:
  0.0 0.0 copy-start
  0.0 1.5 copy-done
  1.5 1.7 bitcast_bitcast_fusion
  3.2 0.0 copy-start.12
  3.2 6.7 %all-to-all-start = ((bf16[16,448,128]{2,1,0:T(8,128)(2,1)}), bf16[16,448,128]{2,1,0:T(8,128)(2,1)S(1)}, u32[]{:S(2)}, u32[]{:S(2)}) async-start(bf16[16,448,128]{2,1,0:T(8,128)(2,1)} %bitcast_bitcast_fusion), calls=%async_computation | async-start | bytes 3670016 | tf_op jit(solution)/shard_map/all_to_all | solution.py:316
  9.9 0.0 copy-done.12
  9.9 0.6 reshape.50.gain_ref
  10.5 41.2 %all-to-all-done = bf16[16,448,128]{2,1,0:T(8,128)(2,1)S(1)} async-done(((bf16[16,448,128]{2,1,0:T(8,128)(2,1)}), bf16[16,448,128]{2,1,0:T(8,128)(2,1)S(1)}, u32[]{:S(2)}, u32[]{:S(2)}) %all-to-all-start) | async-done | bytes 1835040 | tf_op jit(solution)/shard_map/all_to_all | solution.py:316
  51.7 0.0 copy-start.2
  51.7 1.2 copy-done.2
  52.9 6.4 %first.1 = (f32[8,128]{1,0:T(8,128)}, bf16[128,7168]{1,0:T(8,128)(2,1)}, bf16[128,7168]{1,0:T(8,128)(2,1)}) custom-call(bf16[7168,128]{1,0:T(8,128)(2,1)} %bitcast.24, bf16[128,7168]{1,0:T(8,128)(2,1)} %res_ref.3, bf16[1,7168]{1,0:T(2,128)(2,1)} %reshape.50.gain_ref, bf16[16,7168]{1,0:T(8,128)(2,1)} %bitcast.40, s32[2,128]{1,0:T(2,128)} %bitcast.41), custom_call_target="tpu_custom_call" | custom-call | flops 234881024 | bytes 9175040 | tf_op jit(solution)/shard_map/first/pallas_call | solution.py:96
  59.4 4.9 %all-to-all-start.1 = ((bf16[16,8,7168]{2,1,0:T(8,128)(2,1)}), bf16[16,8,7168]{2,1,0:T(8,128)(2,1)S(1)}, u32[]{:S(2)}, u32[]{:S(2)}) async-start(bf16[16,8,7168]{2,1,0:T(8,128)(2,1)} %bitcast.38), calls=%async_computation.1 | async-start | bytes 3670016 | tf_op jit(solution)/shard_map/all_to_all | solution.py:311
  64.3 6.0 %others.1 = (f32[128,7168]{1,0:T(8,128)}, bf16[128,7168]{1,0:T(8,128)(2,1)}, bf16[128,3584]{1,0:T(8,128)(2,1)}) custom-call(bf16[7168,128]{1,0:T(8,128)(2,1)} %bitcast.25, bf16[128,7168]{1,0:T(8,128)(2,1)} %res_ref.3, f32[8,128]{1,0:T(8,128)} %get-tuple-element.26.aux_ref, bf16[128,7168]{1,0:T(8,128)(2,1)} %get-tuple-element.27.normed_ref), custom_call_target="tpu_custom_call" | custom-call | flops 469762048 | bytes 12845056 | tf_op jit(solution)/shard_map/others/pallas_call | solution.py:124
  70.2 35.8 %all-to-all-done.1 = bf16[16,8,7168]{2,1,0:T(8,128)(2,1)S(1)} async-done(((bf16[16,8,7168]{2,1,0:T(8,128)(2,1)}), bf16[16,8,7168]{2,1,0:T(8,128)(2,1)S(1)}, u32[]{:S(2)}, u32[]{:S(2)}) %all-to-all-start.1) | async-done | bytes 1835040 | tf_op jit(solution)/shard_map/all_to_all | solution.py:311
  106.1 0.0 copy-start.4
  106.1 1.2 copy-done.4
  107.3 4.9 %all-to-all-start.2 = ((bf16[16,8,7168]{2,1,0:T(8,128)(2,1)}), bf16[16,8,7168]{2,1,0:T(8,128)(2,1)S(1)}, u32[]{:S(2)}, u32[]{:S(2)}) async-start(bf16[16,8,7168]{2,1,0:T(8,128)(2,1)} %bitcast.37), calls=%async_computation.2 | async-start | bytes 3670016 | tf_op jit(solution)/shard_map/all_to_all | solution.py:311
  112.2 1.2 collective-permute-start
  113.5 41.0 %all-to-all-done.2 = bf16[16,8,7168]{2,1,0:T(8,128)(2,1)S(1)} async-done(((bf16[16,8,7168]{2,1,0:T(8,128)(2,1)}), bf16[16,8,7168]{2,1,0:T(8,128)(2,1)S(1)}, u32[]{:S(2)}, u32[]{:S(2)}) %all-to-all-start.2) | async-done | bytes 1835040 | tf_op jit(solution)/shard_map/all_to_all | solution.py:311
  154.4 0.0 copy-start.3
  154.4 1.2 collective-permute-start.2
  155.7 0.0 collective-permute-done.refs_1_
  155.7 9.4 %inward.3.refs_0_ = bf16[256,512]{1,0:T(8,128)(2,1)} custom-call(bf16[128,7168]{1,0:T(8,128)(2,1)} %bitcast.29, bf16[128,7168]{1,0:T(8,128)(2,1)} %collective-permute-done.refs_1_, bf16[1,7168,512]{2,1,0:T(8,128)(2,1)} %refs_2_.10, bf16[1,7168,512]{2,1,0:T(8,128)(2,1)} %refs_3_.5), custom_call_target="tpu_custom_call" | custom-call | flops 256 | bytes 256 | tf_op jit(solution)/shard_map/inward/pallas_call | solution.py:169
  165.1 0.0 copy-done.3
  165.1 0.0 copy-start.8
  165.1 5.1 %all-to-all-start.3 = ((bf16[16,8,3584]{2,1,0:T(8,128)(2,1)}), bf16[16,8,3584]{2,1,0:T(8,128)(2,1)S(1)}, u32[]{:S(2)}, u32[]{:S(2)}) async-start(bf16[16,8,3584]{2,1,0:T(8,128)(2,1)} %bitcast.39), calls=%async_computation.3 | async-start | bytes 1835008 | tf_op jit(solution)/shard_map/all_to_all | solution.py:311
  170.2 0.0 copy-done.8
  170.2 1.3 collective-permute-start.1
  171.5 30.3 %collective-permute-done.1.refs_1_ = bf16[256,512]{1,0:T(8,128)(2,1)S(1)} collective-permute-done((bf16[256,512]{1,0:T(8,128)(2,1)S(1)}, bf16[256,512]{1,0:T(8,128)(2,1)S(1)}, u32[]{:S(2)}, u32[]{:S(2)}) %collective-permute-start.1) | collective-permute-done | bytes 262176 | tf_op jit(solution)/shard_map/ppermute | solution.py:307
  201.8 0.0 copy-start.9
  201.8 0.7 copy-done.9
  202.5 6.4 %outward.3 = bf16[2,128,3584]{2,1,0:T(8,128)(2,1)} custom-call(s32[1]{0:T(128)} %bitcast.5.here_ref, bf16[256,512]{1,0:T(8,128)(2,1)} %inward.3.refs_0_, bf16[256,512]{1,0:T(8,128)(2,1)} %copy-done.9, bf16[1,3584,1024]{2,1,0:T(8,128)(2,1)} %refs_2_.11), custom_call_target="tpu_custom_call" | custom-call | flops 256 | bytes 256 | tf_op jit(solution)/shard_map/outward/pallas_call | solution.py:234
  208.9 0.0 collective-permute-done.2.refs_1_
  209.0 0.0 all-to-all-done.3
  209.0 0.0 copy-start.6
  209.0 4.8 %all-to-all-start.4 = ((bf16[32,8,3584]{2,1,0:T(8,128)(2,1)}), bf16[32,8,3584]{2,1,0:T(8,128)(2,1)S(1)}, u32[]{:S(2)}, u32[]{:S(2)}) async-start(bf16[32,8,3584]{2,1,0:T(8,128)(2,1)} %bitcast.30), calls=%async_computation.4 | async-start | bytes 3670016 | tf_op jit(solution)/shard_map/all_to_all | solution.py:324
  213.7 9.4 %inward.4.refs_0_ = bf16[256,512]{1,0:T(8,128)(2,1)} custom-call(bf16[128,7168]{1,0:T(8,128)(2,1)} %bitcast.27, bf16[128,7168]{1,0:T(8,128)(2,1)} %collective-permute-done.2.refs_1_, bf16[1,7168,512]{2,1,0:T(8,128)(2,1)} %refs_2_.10, bf16[1,7168,512]{2,1,0:T(8,128)(2,1)} %refs_3_.5), custom_call_target="tpu_custom_call" | custom-call | flops 256 | bytes 256 | tf_op jit(solution)/shard_map/inward/pallas_call | solution.py:169
  223.2 1.2 collective-permute-start.3
  224.3 11.8 %collective-permute-done.3.refs_1_ = bf16[256,512]{1,0:T(8,128)(2,1)S(1)} collective-permute-done((bf16[256,512]{1,0:T(8,128)(2,1)}, bf16[256,512]{1,0:T(8,128)(2,1)S(1)}, u32[]{:S(2)}, u32[]{:S(2)}) %collective-permute-start.3) | collective-permute-done | bytes 262176 | tf_op jit(solution)/shard_map/ppermute | solution.py:307
  236.2 0.0 copy-done.6
  236.2 0.0 copy-start.10
  236.2 0.1 collective-permute-start.4
  236.3 0.6 copy-done.10
  236.9 6.5 %outward.4 = bf16[2,128,3584]{2,1,0:T(8,128)(2,1)} custom-call(s32[1]{0:T(128)} %bitcast.5.here_ref, bf16[256,512]{1,0:T(8,128)(2,1)} %inward.4.refs_0_, bf16[256,512]{1,0:T(8,128)(2,1)} %copy-done.10, bf16[1,3584,1024]{2,1,0:T(8,128)(2,1)} %refs_2_.11), custom_call_target="tpu_custom_call" | custom-call | flops 256 | bytes 256 | tf_op jit(solution)/shard_map/outward/pallas_call | solution.py:234
  243.3 21.0 %collective-permute-done.4.refs_1_ = bf16[128,3584]{1,0:T(8,128)(2,1)} collective-permute-done((bf16[128,3584]{1,0:T(8,128)(2,1)S(1)}, bf16[128,3584]{1,0:T(8,128)(2,1)}, u32[]{:S(2)}, u32[]{:S(2)}) %collective-permute-start.4) | collective-permute-done | bytes 917536 | tf_op jit(solution)/shard_map/ppermute | solution.py:307
  264.3 0.0 all-to-all-done.4
  264.3 0.0 copy-start.5
  264.3 1.2 copy-done.5
  265.5 4.4 %all-to-all-start.5 = ((bf16[32,8,3584]{2,1,0:T(8,128)(2,1)}), bf16[32,8,3584]{2,1,0:T(8,128)(2,1)}, u32[]{:S(2)}, u32[]{:S(2)}) async-start(bf16[32,8,3584]{2,1,0:T(8,128)(2,1)} %bitcast.31), calls=%async_computation.5 | async-start | bytes 3670016 | tf_op jit(solution)/shard_map/all_to_all | solution.py:324
  269.9 8.7 %inward.5.refs_0_ = bf16[128,512]{1,0:T(8,128)(2,1)} custom-call(bf16[128,3584]{1,0:T(8,128)(2,1)} %bitcast.35, bf16[128,3584]{1,0:T(8,128)(2,1)} %collective-permute-done.4.refs_1_, bf16[1,7168,512]{2,1,0:T(8,128)(2,1)} %refs_2_.10, bf16[1,7168,512]{2,1,0:T(8,128)(2,1)} %refs_3_.5), custom_call_target="tpu_custom_call" | custom-call | flops 128 | bytes 128 | tf_op jit(solution)/shard_map/inward/pallas_call | solution.py:169
  278.6 1.2 collective-permute-start.5
  279.8 7.5 %collective-permute-done.5.refs_1_ = bf16[128,512]{1,0:T(8,128)(2,1)S(1)} collective-permute-done((bf16[128,512]{1,0:T(8,128)(2,1)}, bf16[128,512]{1,0:T(8,128)(2,1)S(1)}, u32[]{:S(2)}, u32[]{:S(2)}) %collective-permute-start.5) | collective-permute-done | bytes 131104 | tf_op jit(solution)/shard_map/ppermute | solution.py:307
  287.3 0.0 copy-start.11
  287.3 0.6 copy-done.11
  287.9 7.5 %outward.5 = bf16[2,128,1792]{2,1,0:T(8,128)(2,1)} custom-call(s32[1]{0:T(128)} %bitcast.5.here_ref, bf16[128,512]{1,0:T(8,128)(2,1)} %inward.5.refs_0_, bf16[128,512]{1,0:T(8,128)(2,1)} %copy-done.11, bf16[1,3584,1024]{2,1,0:T(8,128)(2,1)} %refs_2_.11), custom_call_target="tpu_custom_call" | custom-call | flops 128 | bytes 128 | tf_op jit(solution)/shard_map/outward/pallas_call | solution.py:234
  295.4 15.1 %all-to-all-done.5 = bf16[32,8,3584]{2,1,0:T(8,128)(2,1)} async-done(((bf16[32,8,3584]{2,1,0:T(8,128)(2,1)}), bf16[32,8,3584]{2,1,0:T(8,128)(2,1)}, u32[]{:S(2)}, u32[]{:S(2)}) %all-to-all-start.5) | async-done | bytes 1835040 | tf_op jit(solution)/shard_map/all_to_all | solution.py:324
  310.5 6.1 %all-to-all-start.6 = ((bf16[32,8,1792]{2,1,0:T(8,128)(2,1)}), bf16[32,8,1792]{2,1,0:T(8,128)(2,1)S(1)}, u32[]{:S(2)}, u32[]{:S(2)}) async-start(bf16[32,8,1792]{2,1,0:T(8,128)(2,1)} %bitcast.33), calls=%async_computation.6 | async-start | bytes 1835008 | tf_op jit(solution)/shard_map/all_to_all | solution.py:324
  316.6 4.7 %combine.3.stream_ref = f32[128,7168]{1,0:T(8,128)} custom-call(f32[8,128]{1,0:T(8,128)} %get-tuple-element.26.aux_ref, f32[128,7168]{1,0:T(8,128)} %get-tuple-element.28.stream_ref, bf16[2,128,3584]{2,1,0:T(8,128)(2,1)} %bitcast.32), custom_call_target="tpu_custom_call" | custom-call | flops 469762048 | bytes 9175040 | tf_op jit(solution)/shard_map/combine/pallas_call | solution.py:269
  321.4 4.7 %combine.4.stream_ref = f32[128,7168]{1,0:T(8,128)} custom-call(f32[8,128]{1,0:T(8,128)} %get-tuple-element.26.aux_ref, f32[128,7168]{1,0:T(8,128)} %combine.3.stream_ref, bf16[2,128,3584]{2,1,0:T(8,128)(2,1)} %bitcast.15.back_ref), custom_call_target="tpu_custom_call" | custom-call | flops 469762048 | bytes 9175040 | tf_op jit(solution)/shard_map/combine/pallas_call | solution.py:269
  326.1 12.7 %all-to-all-done.6 = bf16[32,8,1792]{2,1,0:T(8,128)(2,1)S(1)} async-done(((bf16[32,8,1792]{2,1,0:T(8,128)(2,1)}), bf16[32,8,1792]{2,1,0:T(8,128)(2,1)S(1)}, u32[]{:S(2)}, u32[]{:S(2)}) %all-to-all-start.6) | async-done | bytes 917536 | tf_op jit(solution)/shard_map/all_to_all | solution.py:324
  338.8 0.0 copy-start.7
  338.8 0.9 copy-done.7
  339.7 4.3 %combine.5 = bf16[128,7168]{1,0:T(8,128)(2,1)} custom-call(f32[8,128]{1,0:T(8,128)} %get-tuple-element.26.aux_ref, f32[128,7168]{1,0:T(8,128)} %combine.4.stream_ref, bf16[2,128,1792]{2,1,0:T(8,128)(2,1)} %bitcast.36), custom_call_target="tpu_custom_call" | custom-call | flops 469762048 | bytes 8257536 | tf_op jit(solution)/shard_map/combine/pallas_call | solution.py:269
  344.0 0.0 copy-done.1
  (1 shorter events, 0.0 us)
Async XLA Ops:
  0.0 1.5 copy-start
  3.2 6.7 %copy-start.12 = (bf16[7168]{0:T(1024)(128)(2,1)S(1)}, bf16[7168]{0:T(1024)(128)(2,1)}, u32[]{:S(2)}) copy-start(bf16[7168]{0:T(1024)(128)(2,1)} %param.10) | copy-start | bytes 43012
  3.2 48.5 %all-to-all-start = ((bf16[16,448,128]{2,1,0:T(8,128)(2,1)}), bf16[16,448,128]{2,1,0:T(8,128)(2,1)S(1)}, u32[]{:S(2)}, u32[]{:S(2)}) async-start(bf16[16,448,128]{2,1,0:T(8,128)(2,1)} %bitcast_bitcast_fusion), calls=%async_computation | async-start | bytes 3670016 | tf_op jit(solution)/shard_map/all_to_all | solution.py:316
  51.7 1.2 copy-start.2
  59.4 46.7 %all-to-all-start.1 = ((bf16[16,8,7168]{2,1,0:T(8,128)(2,1)}), bf16[16,8,7168]{2,1,0:T(8,128)(2,1)S(1)}, u32[]{:S(2)}, u32[]{:S(2)}) async-start(bf16[16,8,7168]{2,1,0:T(8,128)(2,1)} %bitcast.38), calls=%async_computation.1 | async-start | bytes 3670016 | tf_op jit(solution)/shard_map/all_to_all | solution.py:311
  106.1 1.2 copy-start.4
  107.3 47.1 %all-to-all-start.2 = ((bf16[16,8,7168]{2,1,0:T(8,128)(2,1)}), bf16[16,8,7168]{2,1,0:T(8,128)(2,1)S(1)}, u32[]{:S(2)}, u32[]{:S(2)}) async-start(bf16[16,8,7168]{2,1,0:T(8,128)(2,1)} %bitcast.37), calls=%async_computation.2 | async-start | bytes 3670016 | tf_op jit(solution)/shard_map/all_to_all | solution.py:311
  112.2 43.4 %collective-permute-start = (bf16[128,7168]{1,0:T(8,128)(2,1)}, bf16[128,7168]{1,0:T(8,128)(2,1)}, u32[]{:S(2)}, u32[]{:S(2)}) collective-permute-start(bf16[128,7168]{1,0:T(8,128)(2,1)} %bitcast.28), channel_id=1, source_target_pairs={{0,1},{1,0},{2,3},{3,2},{4,5},{5,4},{6,7},{7,6},{8,9},{9,8},{10,11... | collective-permute-start | bytes 5505032 | tf_op jit(solution)/shard_map/ppermute | solution.py:307
  154.4 10.6 %copy-start.3 = (bf16[16,8,7168]{2,1,0:T(8,128)(2,1)}, bf16[16,8,7168]{2,1,0:T(8,128)(2,1)S(1)}, u32[]{:S(2)}) copy-start(bf16[16,8,7168]{2,1,0:T(8,128)(2,1)S(1)} %all-to-all-done.2) | copy-start | bytes 5505028
  154.4 54.5 %collective-permute-start.2 = (bf16[128,7168]{1,0:T(8,128)(2,1)S(1)}, bf16[128,7168]{1,0:T(8,128)(2,1)}, u32[]{:S(2)}, u32[]{:S(2)}) collective-permute-start(bf16[128,7168]{1,0:T(8,128)(2,1)S(1)} %bitcast.26), channel_id=1, source_target_pairs={{0,1},{1,0},{2,3},{3,2},{4,5},{5,4},{6,7},{7,6},{8,9},{9,8},{10,11... | collective-permute-start | bytes 5505032 | tf_op jit(solution)/shard_map/ppermute | solution.py:307
  165.1 5.1 %copy-start.8 = (bf16[256,512]{1,0:T(8,128)(2,1)S(1)}, bf16[256,512]{1,0:T(8,128)(2,1)}, u32[]{:S(2)}) copy-start(bf16[256,512]{1,0:T(8,128)(2,1)} %inward.3.refs_0_) | copy-start | bytes 786436
  165.1 43.9 %all-to-all-start.3 = ((bf16[16,8,3584]{2,1,0:T(8,128)(2,1)}), bf16[16,8,3584]{2,1,0:T(8,128)(2,1)S(1)}, u32[]{:S(2)}, u32[]{:S(2)}) async-start(bf16[16,8,3584]{2,1,0:T(8,128)(2,1)} %bitcast.39), calls=%async_computation.3 | async-start | bytes 1835008 | tf_op jit(solution)/shard_map/all_to_all | solution.py:311
  170.2 31.6 %collective-permute-start.1 = (bf16[256,512]{1,0:T(8,128)(2,1)S(1)}, bf16[256,512]{1,0:T(8,128)(2,1)S(1)}, u32[]{:S(2)}, u32[]{:S(2)}) collective-permute-start(bf16[256,512]{1,0:T(8,128)(2,1)S(1)} %copy-done.8), channel_id=1, source_target_pairs={{0,1},{1,0},{2,3},{3,2},{4,5},{5,4},{6,7},{7,6},{8,9},{9,8},{10,11... | collective-permute-start | bytes 786440 | tf_op jit(solution)/shard_map/ppermute | solution.py:307
  201.8 0.7 copy-start.9
  209.0 27.2 %copy-start.6 = (bf16[16,8,3584]{2,1,0:T(8,128)(2,1)}, bf16[16,8,3584]{2,1,0:T(8,128)(2,1)S(1)}, u32[]{:S(2)}) copy-start(bf16[16,8,3584]{2,1,0:T(8,128)(2,1)S(1)} %all-to-all-done.3) | copy-start | bytes 2752516
  209.0 55.3 %all-to-all-start.4 = ((bf16[32,8,3584]{2,1,0:T(8,128)(2,1)}), bf16[32,8,3584]{2,1,0:T(8,128)(2,1)S(1)}, u32[]{:S(2)}, u32[]{:S(2)}) async-start(bf16[32,8,3584]{2,1,0:T(8,128)(2,1)} %bitcast.30), calls=%async_computation.4 | async-start | bytes 3670016 | tf_op jit(solution)/shard_map/all_to_all | solution.py:324
  223.2 13.0 %collective-permute-start.3 = (bf16[256,512]{1,0:T(8,128)(2,1)}, bf16[256,512]{1,0:T(8,128)(2,1)S(1)}, u32[]{:S(2)}, u32[]{:S(2)}) collective-permute-start(bf16[256,512]{1,0:T(8,128)(2,1)} %inward.4.refs_0_), channel_id=1, source_target_pairs={{0,1},{1,0},{2,3},{3,2},{4,5},{5,4},{6,7},{7,6},{8,9},{9,8},{10,11... | collective-permute-start | bytes 786440 | tf_op jit(solution)/shard_map/ppermute | solution.py:307
  236.2 0.7 copy-start.10
  236.2 28.1 %collective-permute-start.4 = (bf16[128,3584]{1,0:T(8,128)(2,1)S(1)}, bf16[128,3584]{1,0:T(8,128)(2,1)}, u32[]{:S(2)}, u32[]{:S(2)}) collective-permute-start(bf16[128,3584]{1,0:T(8,128)(2,1)S(1)} %bitcast.34), channel_id=1, source_target_pairs={{0,1},{1,0},{2,3},{3,2},{4,5},{5,4},{6,7},{7,6},{8,9},{9,8},{10,11... | collective-permute-start | bytes 2752520 | tf_op jit(solution)/shard_map/ppermute | solution.py:307
  264.3 1.2 copy-start.5
  265.5 45.0 %all-to-all-start.5 = ((bf16[32,8,3584]{2,1,0:T(8,128)(2,1)}), bf16[32,8,3584]{2,1,0:T(8,128)(2,1)}, u32[]{:S(2)}, u32[]{:S(2)}) async-start(bf16[32,8,3584]{2,1,0:T(8,128)(2,1)} %bitcast.31), calls=%async_computation.5 | async-start | bytes 3670016 | tf_op jit(solution)/shard_map/all_to_all | solution.py:324
  278.6 8.7 %collective-permute-start.5 = (bf16[128,512]{1,0:T(8,128)(2,1)}, bf16[128,512]{1,0:T(8,128)(2,1)S(1)}, u32[]{:S(2)}, u32[]{:S(2)}) collective-permute-start(bf16[128,512]{1,0:T(8,128)(2,1)} %inward.5.refs_0_), channel_id=1, source_target_pairs={{0,1},{1,0},{2,3},{3,2},{4,5},{5,4},{6,7},{7,6},{8,9},{9,8},{10,11... | collective-permute-start | bytes 393224 | tf_op jit(solution)/shard_map/ppermute | solution.py:307
  287.3 0.7 copy-start.11
  310.5 28.2 %all-to-all-start.6 = ((bf16[32,8,1792]{2,1,0:T(8,128)(2,1)}), bf16[32,8,1792]{2,1,0:T(8,128)(2,1)S(1)}, u32[]{:S(2)}, u32[]{:S(2)}) async-start(bf16[32,8,1792]{2,1,0:T(8,128)(2,1)} %bitcast.33), calls=%async_computation.6 | async-start | bytes 1835008 | tf_op jit(solution)/shard_map/all_to_all | solution.py:324
  338.8 0.9 copy-start.7
  338.8 5.2 %copy-start.1 = (bf16[2048,448]{0,1:T(8,128)(2,1)S(1)}, bf16[2048,448]{0,1:T(8,128)(2,1)}, u32[]{:S(2)}) copy-start(bf16[2048,448]{0,1:T(8,128)(2,1)} %param.8) | copy-start | bytes 5505028

commit v3 on v2

--- a/solution.py
+++ b/solution.py
@@ -147,11 +147,14 @@
     pieces = [ref[...] for ref in piece_refs]
     if fold > 1:
         part = step // (STEPS // fold)
-        rows = pieces[0].shape[0]
-        out_row = lax.broadcasted_iota(jnp.int32, (rows // fold, rows), 0)
-        in_row = lax.broadcasted_iota(jnp.int32, (rows // fold, rows), 1)
-        select = as_mask(in_row == (out_row // few) * base + part * few + out_row % few)
-        pieces = [dot(select, piece).astype(BF16) for piece in pieces]
+        unfolded = []
+        for piece in pieces:
+            rows = piece.shape[0]
+            out_row = lax.broadcasted_iota(jnp.int32, (rows // fold, rows), 0)
+            in_row = lax.broadcasted_iota(jnp.int32, (rows // fold, rows), 1)
+            select = as_mask(in_row == (out_row // few) * base + part * few + out_row % few)
+            unfolded.append(dot(select, piece).astype(BF16))
+        pieces = unfolded
     block = jnp.concatenate(pieces, axis=0)
     acc[:, :ff] += dot(block, gate_ref[0])
     acc[:, ff:] += dot(block, up_ref[0])
@@ -302,9 +305,10 @@
     cols = down_weight.shape[1]
     here = lax.axis_index("blk").astype(jnp.int32).reshape(1)
 
-    def shared(block):
+    def shared(block, cuts=1):
         shifts = [[(i, (i + o) % parts) for i in range(parts)] for o in range(1, parts)]
-        return [block] + [lax.ppermute(block, "blk", perm) for perm in shifts]
+        sent = jnp.split(block, cuts, axis=0)
+        return [block] + [lax.ppermute(piece, "blk", perm) for perm in shifts for piece in sent]
 
     def dispatch(pack):
         pack = pack.reshape(groups, base, -1)
@@ -344,9 +348,9 @@
     back_a = returned(made)
     hidden = shared(gate_up(1, pieces_b))
     hidden, arrived_c = tie((hidden, arrived_c))
-    pieces_c = shared(arrived_c)
+    pieces_c = shared(arrived_c, 2)
     made = down(1, hidden)
-    made, pieces_c = tie((made, pieces_c))
+    made, pieces_c[1::2] = tie((made, pieces_c[1::2]))
     back_b = returned(made)
     back_c = returned(down(2, shared(gate_up(2, pieces_c))))
     for group, back in enumerate((back_a, back_b, back_c)):

time: 348 us -> 352 us (1.011)
  starting transfers between devices: 43.1 us -> 47.4 us
    all_to_all x3, waiting for transfers between devices: 27.8 us -> 12.7 us  [returned(): lax.all_to_all(made, ('blk', 'dp'), split_axis=0, concat_axis=0, tiled=True)]
    ppermute x6 -> x7, waiting for transfers between devices: 70.6 us -> 84.3 us  [shared(): lax.ppermute(piece, 'blk', perm)]
    all_to_all x3, starting transfers between devices: 15.2 us -> 19.1 us  [returned(): lax.all_to_all(made, ('blk', 'dp'), split_axis=0, concat_axis=0, tiled=True)]
    unnamed x26 -> x30, local copies, waits for them, and re-layouts: 8.06 us -> 8.81 us
  transfers between devices with their start and end apart: 13 -> 14, of which waited for: 9 -> 10; matrix products, arithmetic and copies ran while one was open for 0% -> 0% of each run, Pallas kernels for 18% -> 18%
where the time goes in v3:
time: 352 us; the launch traced here: 348 us
  waiting for transfers between devices  215 us (61%)
  Pallas kernels  74.1 us (21%)
  starting transfers between devices  47.4 us (13%)
  local copies, waits for them, and re-layouts  11.2 us (3%)
    ppermute x7, waiting for transfers between devices, shared(): lax.ppermute(piece, 'blk', perm)  84.3 us
    all_to_all x3, waiting for transfers between devices, dispatch(): got = lax.all_to_all(pack, 'dp', split_axis=0, concat_axis=0, tiled=True)  76.8 us
    all_to_all x1, waiting for transfers between devices, body(): attn = lax.all_to_all(send, 'dp', split_axis=0, concat_axis=0, tiled=True)  41.2 us
    pallas_call x3, Pallas kernels, inward(): pl.pallas_call(functools.partial(inward_kernel, base, fold, len(pieces)),...  27.6 us
    pallas_call x3, Pallas kernels, outward(): pl.pallas_call(functools.partial(outward_kernel, base, fold, parts), grid...  20.4 us
    all_to_all x3, starting transfers between devices, returned(): lax.all_to_all(made, ('blk', 'dp'), split_axis=0, concat_axis=0, tiled=True)  19.1 us
    all_to_all x3, starting transfers between devices, dispatch(): got = lax.all_to_all(pack, 'dp', split_axis=0, concat_axis=0, tiled=True)  14.9 us
    pallas_call x3, Pallas kernels, combine(): pl.pallas_call(functools.partial(combine_kernel, base, fold, back_fold, g...  13.8 us
  transfers between devices with their start and end apart: 14, of which 10 were waited for; matrix products, arithmetic and copies ran while one was open for 0% of the time, Pallas kernels for 18%

profile of v3, /device:TPU:11, one launch (start us, length us, event | category | flops | bytes accessed | tf_op | source)
XLA Modules:
  0.0 347.8 jit_solution(1534813472318310645)
XLA Ops:
  0.0 0.0 copy-start
  0.0 1.5 copy-done
  1.5 1.7 bitcast_bitcast_fusion
  3.2 0.0 copy-start.14
  3.2 6.7 %all-to-all-start = ((bf16[16,448,128]{2,1,0:T(8,128)(2,1)}), bf16[16,448,128]{2,1,0:T(8,128)(2,1)S(1)}, u32[]{:S(2)}, u32[]{:S(2)}) async-start(bf16[16,448,128]{2,1,0:T(8,128)(2,1)} %bitcast_bitcast_fusion), calls=%async_computation | async-start | bytes 3670016 | tf_op jit(solution)/shard_map/all_to_all | solution.py:320
  9.9 0.0 copy-done.14
  9.9 0.6 reshape.50.gain_ref
  10.5 41.2 %all-to-all-done = bf16[16,448,128]{2,1,0:T(8,128)(2,1)S(1)} async-done(((bf16[16,448,128]{2,1,0:T(8,128)(2,1)}), bf16[16,448,128]{2,1,0:T(8,128)(2,1)S(1)}, u32[]{:S(2)}, u32[]{:S(2)}) %all-to-all-start) | async-done | bytes 1835040 | tf_op jit(solution)/shard_map/all_to_all | solution.py:320
  51.7 0.0 copy-start.2
  51.7 1.2 copy-done.2
  52.9 6.4 %first.1 = (f32[8,128]{1,0:T(8,128)}, bf16[128,7168]{1,0:T(8,128)(2,1)}, bf16[128,7168]{1,0:T(8,128)(2,1)}) custom-call(bf16[7168,128]{1,0:T(8,128)(2,1)} %bitcast.24, bf16[128,7168]{1,0:T(8,128)(2,1)} %res_ref.3, bf16[1,7168]{1,0:T(2,128)(2,1)} %reshape.50.gain_ref, bf16[16,7168]{1,0:T(8,128)(2,1)} %bitcast.40, s32[2,128]{1,0:T(2,128)} %bitcast.41), custom_call_target="tpu_custom_call" | custom-call | flops 234881024 | bytes 9175040 | tf_op jit(solution)/shard_map/first/pallas_call | solution.py:96
  59.3 4.9 %all-to-all-start.1 = ((bf16[16,8,7168]{2,1,0:T(8,128)(2,1)}), bf16[16,8,7168]{2,1,0:T(8,128)(2,1)S(1)}, u32[]{:S(2)}, u32[]{:S(2)}) async-start(bf16[16,8,7168]{2,1,0:T(8,128)(2,1)} %bitcast.38), calls=%async_computation.1 | async-start | bytes 3670016 | tf_op jit(solution)/shard_map/all_to_all | solution.py:315
  64.3 6.0 %others.1 = (f32[128,7168]{1,0:T(8,128)}, bf16[128,7168]{1,0:T(8,128)(2,1)}, bf16[128,3584]{1,0:T(8,128)(2,1)}) custom-call(bf16[7168,128]{1,0:T(8,128)(2,1)} %bitcast.25, bf16[128,7168]{1,0:T(8,128)(2,1)} %res_ref.3, f32[8,128]{1,0:T(8,128)} %get-tuple-element.25.aux_ref, bf16[128,7168]{1,0:T(8,128)(2,1)} %get-tuple-element.26.normed_ref), custom_call_target="tpu_custom_call" | custom-call | flops 469762048 | bytes 12845056 | tf_op jit(solution)/shard_map/others/pallas_call | solution.py:124
  70.2 35.8 %all-to-all-done.1 = bf16[16,8,7168]{2,1,0:T(8,128)(2,1)S(1)} async-done(((bf16[16,8,7168]{2,1,0:T(8,128)(2,1)}), bf16[16,8,7168]{2,1,0:T(8,128)(2,1)S(1)}, u32[]{:S(2)}, u32[]{:S(2)}) %all-to-all-start.1) | async-done | bytes 1835040 | tf_op jit(solution)/shard_map/all_to_all | solution.py:315
  106.1 0.0 copy-start.5
  106.1 1.2 copy-done.5
  107.3 4.9 %all-to-all-start.2 = ((bf16[16,8,7168]{2,1,0:T(8,128)(2,1)}), bf16[16,8,7168]{2,1,0:T(8,128)(2,1)S(1)}, u32[]{:S(2)}, u32[]{:S(2)}) async-start(bf16[16,8,7168]{2,1,0:T(8,128)(2,1)} %bitcast.37), calls=%async_computation.2 | async-start | bytes 3670016 | tf_op jit(solution)/shard_map/all_to_all | solution.py:315
  112.2 1.2 collective-permute-start
  113.4 41.0 %all-to-all-done.2 = bf16[16,8,7168]{2,1,0:T(8,128)(2,1)S(1)} async-done(((bf16[16,8,7168]{2,1,0:T(8,128)(2,1)}), bf16[16,8,7168]{2,1,0:T(8,128)(2,1)S(1)}, u32[]{:S(2)}, u32[]{:S(2)}) %all-to-all-start.2) | async-done | bytes 1835040 | tf_op jit(solution)/shard_map/all_to_all | solution.py:315
  154.4 1.2 collective-permute-start.2
  155.6 0.0 collective-permute-done.refs_1_
  155.6 9.4 %inward.3.refs_0_ = bf16[256,512]{1,0:T(8,128)(2,1)} custom-call(bf16[128,7168]{1,0:T(8,128)(2,1)} %bitcast.31, bf16[128,7168]{1,0:T(8,128)(2,1)} %collective-permute-done.refs_1_, bf16[1,7168,512]{2,1,0:T(8,128)(2,1)} %refs_3_.5, bf16[1,7168,512]{2,1,0:T(8,128)(2,1)} %refs_4_.1), custom_call_target="tpu_custom_call" | custom-call | flops 256 | bytes 256 | tf_op jit(solution)/shard_map/inward/pallas_call | solution.py:172
  165.0 0.0 copy-done.4
  165.0 0.0 copy-start.8
  165.0 5.1 %all-to-all-start.3 = ((bf16[16,8,3584]{2,1,0:T(8,128)(2,1)}), bf16[16,8,3584]{2,1,0:T(8,128)(2,1)S(1)}, u32[]{:S(2)}, u32[]{:S(2)}) async-start(bf16[16,8,3584]{2,1,0:T(8,128)(2,1)} %bitcast.39), calls=%async_computation.3 | async-start | bytes 1835008 | tf_op jit(solution)/shard_map/all_to_all | solution.py:315
  170.1 0.0 copy-done.8
  170.1 1.3 collective-permute-start.1
  171.4 30.3 %collective-permute-done.1.refs_1_ = bf16[256,512]{1,0:T(8,128)(2,1)S(1)} collective-permute-done((bf16[256,512]{1,0:T(8,128)(2,1)S(1)}, bf16[256,512]{1,0:T(8,128)(2,1)S(1)}, u32[]{:S(2)}, u32[]{:S(2)}) %collective-permute-start.1) | collective-permute-done | bytes 262176 | tf_op jit(solution)/shard_map/ppermute | solution.py:311
  201.8 0.0 copy-start.12
  201.8 0.7 copy-done.12
  202.5 6.4 %outward.3 = bf16[2,128,3584]{2,1,0:T(8,128)(2,1)} custom-call(s32[1]{0:T(128)} %bitcast.5.here_ref, bf16[256,512]{1,0:T(8,128)(2,1)} %inward.3.refs_0_, bf16[256,512]{1,0:T(8,128)(2,1)} %copy-done.12, bf16[1,3584,1024]{2,1,0:T(8,128)(2,1)} %refs_2_.9), custom_call_target="tpu_custom_call" | custom-call | flops 256 | bytes 256 | tf_op jit(solution)/shard_map/outward/pallas_call | solution.py:237
  208.9 0.0 collective-permute-done.2.refs_1_
  208.9 0.0 all-to-all-done.3
  209.0 0.0 copy-start.3
  209.0 4.7 %all-to-all-start.4 = ((bf16[32,8,3584]{2,1,0:T(8,128)(2,1)}), bf16[32,8,3584]{2,1,0:T(8,128)(2,1)S(1)}, u32[]{:S(2)}, u32[]{:S(2)}) async-start(bf16[32,8,3584]{2,1,0:T(8,128)(2,1)} %bitcast.33), calls=%async_computation.4 | async-start | bytes 3670016 | tf_op jit(solution)/shard_map/all_to_all | solution.py:328
  213.7 9.4 %inward.4.refs_0_ = bf16[256,512]{1,0:T(8,128)(2,1)} custom-call(bf16[128,7168]{1,0:T(8,128)(2,1)} %bitcast.29, bf16[128,7168]{1,0:T(8,128)(2,1)} %collective-permute-done.2.refs_1_, bf16[1,7168,512]{2,1,0:T(8,128)(2,1)} %refs_3_.5, bf16[1,7168,512]{2,1,0:T(8,128)(2,1)} %refs_4_.1), custom_call_target="tpu_custom_call" | custom-call | flops 256 | bytes 256 | tf_op jit(solution)/shard_map/inward/pallas_call | solution.py:172
  223.1 1.2 collective-permute-start.3
  224.3 11.8 %collective-permute-done.3.refs_1_ = bf16[256,512]{1,0:T(8,128)(2,1)S(1)} collective-permute-done((bf16[256,512]{1,0:T(8,128)(2,1)}, bf16[256,512]{1,0:T(8,128)(2,1)S(1)}, u32[]{:S(2)}, u32[]{:S(2)}) %collective-permute-start.3) | collective-permute-done | bytes 262176 | tf_op jit(solution)/shard_map/ppermute | solution.py:311
  236.2 0.0 copy-done.3
  236.2 0.1 fusion
  236.2 0.2 collective-permute-start.4
  236.4 0.5 copy-done.11
  236.9 6.4 %outward.4 = bf16[2,128,3584]{2,1,0:T(8,128)(2,1)} custom-call(s32[1]{0:T(128)} %bitcast.5.here_ref, bf16[256,512]{1,0:T(8,128)(2,1)} %inward.4.refs_0_, bf16[256,512]{1,0:T(8,128)(2,1)} %copy-done.11, bf16[1,3584,1024]{2,1,0:T(8,128)(2,1)} %refs_2_.9), custom_call_target="tpu_custom_call" | custom-call | flops 256 | bytes 256 | tf_op jit(solution)/shard_map/outward/pallas_call | solution.py:237
  243.4 10.7 %collective-permute-done.4.refs_1_ = bf16[64,3584]{1,0:T(8,128)(2,1)S(1)} collective-permute-done((bf16[64,3584]{1,0:T(8,128)(2,1)S(1)}, bf16[64,3584]{1,0:T(8,128)(2,1)S(1)}, u32[]{:S(2)}, u32[]{:S(2)}) %collective-permute-start.4) | collective-permute-done | bytes 458784 | tf_op jit(solution)/shard_map/ppermute | solution.py:311
  254.1 0.2 all-to-all-done.4
  254.3 0.6 copy-done.9
  254.8 0.7 copy-done.6
  255.5 6.9 %all-to-all-start.5 = ((bf16[32,8,3584]{2,1,0:T(8,128)(2,1)}), bf16[32,8,3584]{2,1,0:T(8,128)(2,1)}, u32[]{:S(2)}, u32[]{:S(2)}) async-start(bf16[32,8,3584]{2,1,0:T(8,128)(2,1)} %bitcast.32), calls=%async_computation.5 | async-start | bytes 3670016 | tf_op jit(solution)/shard_map/all_to_all | solution.py:328
  262.4 1.3 collective-permute-start.5
  263.6 25.5 %collective-permute-done.5.refs_2_ = bf16[64,3584]{1,0:T(8,128)(2,1)S(1)} collective-permute-done((bf16[64,3584]{1,0:T(8,128)(2,1)S(1)}, bf16[64,3584]{1,0:T(8,128)(2,1)S(1)}, u32[]{:S(2)}, u32[]{:S(2)}) %collective-permute-start.5) | collective-permute-done | bytes 458784 | tf_op jit(solution)/shard_map/ppermute | solution.py:311
  289.2 0.8 copy-done.10
  289.9 8.8 %inward.5.refs_0_ = bf16[128,512]{1,0:T(8,128)(2,1)} custom-call(bf16[128,3584]{1,0:T(8,128)(2,1)} %bitcast.27, bf16[64,3584]{1,0:T(8,128)(2,1)} %copy-done.9, bf16[64,3584]{1,0:T(8,128)(2,1)} %copy-done.10, bf16[1,7168,512]{2,1,0:T(8,128)(2,1)} %refs_3_.5, bf16[1,7168,512]{2,1,0:T(8,128)(2,1)} %refs_4_.1), custom_call_target="tpu_custom_call" | custom-call | flops 128 | bytes 128 | tf_op jit(solution)/shard_map/inward/pallas_call | solution.py:172
  298.7 0.3 collective-permute-start.6
  299.0 5.9 %collective-permute-done.6.refs_1_ = bf16[128,512]{1,0:T(8,128)(2,1)S(1)} collective-permute-done((bf16[128,512]{1,0:T(8,128)(2,1)}, bf16[128,512]{1,0:T(8,128)(2,1)S(1)}, u32[]{:S(2)}, u32[]{:S(2)}) %collective-permute-start.6) | collective-permute-done | bytes 131104 | tf_op jit(solution)/shard_map/ppermute | solution.py:311
  304.9 0.7 copy-done.13
  305.6 7.5 %outward.5 = bf16[2,128,1792]{2,1,0:T(8,128)(2,1)} custom-call(s32[1]{0:T(128)} %bitcast.5.here_ref, bf16[128,512]{1,0:T(8,128)(2,1)} %inward.5.refs_0_, bf16[128,512]{1,0:T(8,128)(2,1)} %copy-done.13, bf16[1,3584,1024]{2,1,0:T(8,128)(2,1)} %refs_2_.9), custom_call_target="tpu_custom_call" | custom-call | flops 128 | bytes 128 | tf_op jit(solution)/shard_map/outward/pallas_call | solution.py:237
  313.0 0.0 all-to-all-done.5
  313.0 7.5 %all-to-all-start.6 = ((bf16[32,8,1792]{2,1,0:T(8,128)(2,1)}), bf16[32,8,1792]{2,1,0:T(8,128)(2,1)S(1)}, u32[]{:S(2)}, u32[]{:S(2)}) async-start(bf16[32,8,1792]{2,1,0:T(8,128)(2,1)} %bitcast.35), calls=%async_computation.6 | async-start | bytes 1835008 | tf_op jit(solution)/shard_map/all_to_all | solution.py:328
  320.6 4.7 %combine.3.stream_ref = f32[128,7168]{1,0:T(8,128)} custom-call(f32[8,128]{1,0:T(8,128)} %get-tuple-element.25.aux_ref, f32[128,7168]{1,0:T(8,128)} %get-tuple-element.27.stream_ref, bf16[2,128,3584]{2,1,0:T(8,128)(2,1)} %bitcast.34), custom_call_target="tpu_custom_call" | custom-call | flops 469762048 | bytes 9175040 | tf_op jit(solution)/shard_map/combine/pallas_call | solution.py:272
  325.3 4.8 %combine.4.stream_ref = f32[128,7168]{1,0:T(8,128)} custom-call(f32[8,128]{1,0:T(8,128)} %get-tuple-element.25.aux_ref, f32[128,7168]{1,0:T(8,128)} %combine.3.stream_ref, bf16[2,128,3584]{2,1,0:T(8,128)(2,1)} %bitcast.15.back_ref), custom_call_target="tpu_custom_call" | custom-call | flops 469762048 | bytes 9175040 | tf_op jit(solution)/shard_map/combine/pallas_call | solution.py:272
  330.1 12.5 %all-to-all-done.6 = bf16[32,8,1792]{2,1,0:T(8,128)(2,1)S(1)} async-done(((bf16[32,8,1792]{2,1,0:T(8,128)(2,1)}), bf16[32,8,1792]{2,1,0:T(8,128)(2,1)S(1)}, u32[]{:S(2)}, u32[]{:S(2)}) %all-to-all-start.6) | async-done | bytes 917536 | tf_op jit(solution)/shard_map/all_to_all | solution.py:328
  342.6 0.9 copy-done.7
  343.6 4.3 %combine.5 = bf16[128,7168]{1,0:T(8,128)(2,1)} custom-call(f32[8,128]{1,0:T(8,128)} %get-tuple-element.25.aux_ref, f32[128,7168]{1,0:T(8,128)} %combine.4.stream_ref, bf16[2,128,1792]{2,1,0:T(8,128)(2,1)} %bitcast.36), custom_call_target="tpu_custom_call" | custom-call | flops 469762048 | bytes 8257536 | tf_op jit(solution)/shard_map/combine/pallas_call | solution.py:272
  347.8 0.0 copy-done.1
  (8 shorter events, 0.0 us)
Async XLA Ops:
  0.0 1.5 copy-start
  3.2 6.7 %copy-start.14 = (bf16[7168]{0:T(1024)(128)(2,1)S(1)}, bf16[7168]{0:T(1024)(128)(2,1)}, u32[]{:S(2)}) copy-start(bf16[7168]{0:T(1024)(128)(2,1)} %param.10) | copy-start | bytes 43012
  3.2 48.5 %all-to-all-start = ((bf16[16,448,128]{2,1,0:T(8,128)(2,1)}), bf16[16,448,128]{2,1,0:T(8,128)(2,1)S(1)}, u32[]{:S(2)}, u32[]{:S(2)}) async-start(bf16[16,448,128]{2,1,0:T(8,128)(2,1)} %bitcast_bitcast_fusion), calls=%async_computation | async-start | bytes 3670016 | tf_op jit(solution)/shard_map/all_to_all | solution.py:320
  51.7 1.2 copy-start.2
  59.3 46.7 %all-to-all-start.1 = ((bf16[16,8,7168]{2,1,0:T(8,128)(2,1)}), bf16[16,8,7168]{2,1,0:T(8,128)(2,1)S(1)}, u32[]{:S(2)}, u32[]{:S(2)}) async-start(bf16[16,8,7168]{2,1,0:T(8,128)(2,1)} %bitcast.38), calls=%async_computation.1 | async-start | bytes 3670016 | tf_op jit(solution)/shard_map/all_to_all | solution.py:315
  106.1 1.2 copy-start.5
  107.3 47.1 %all-to-all-start.2 = ((bf16[16,8,7168]{2,1,0:T(8,128)(2,1)}), bf16[16,8,7168]{2,1,0:T(8,128)(2,1)S(1)}, u32[]{:S(2)}, u32[]{:S(2)}) async-start(bf16[16,8,7168]{2,1,0:T(8,128)(2,1)} %bitcast.37), calls=%async_computation.2 | async-start | bytes 3670016 | tf_op jit(solution)/shard_map/all_to_all | solution.py:315
  112.2 43.4 %collective-permute-start = (bf16[128,7168]{1,0:T(8,128)(2,1)}, bf16[128,7168]{1,0:T(8,128)(2,1)}, u32[]{:S(2)}, u32[]{:S(2)}) collective-permute-start(bf16[128,7168]{1,0:T(8,128)(2,1)} %bitcast.30), channel_id=1, source_target_pairs={{0,1},{1,0},{2,3},{3,2},{4,5},{5,4},{6,7},{7,6},{8,9},{9,8},{10,11... | collective-permute-start | bytes 5505032 | tf_op jit(solution)/shard_map/ppermute | solution.py:311
  154.4 10.6 %copy-start.4 = (bf16[16,8,7168]{2,1,0:T(8,128)(2,1)}, bf16[16,8,7168]{2,1,0:T(8,128)(2,1)S(1)}, u32[]{:S(2)}) copy-start(bf16[16,8,7168]{2,1,0:T(8,128)(2,1)S(1)} %all-to-all-done.2) | copy-start | bytes 5505028
  154.4 54.6 %collective-permute-start.2 = (bf16[128,7168]{1,0:T(8,128)(2,1)S(1)}, bf16[128,7168]{1,0:T(8,128)(2,1)}, u32[]{:S(2)}, u32[]{:S(2)}) collective-permute-start(bf16[128,7168]{1,0:T(8,128)(2,1)S(1)} %bitcast.28), channel_id=1, source_target_pairs={{0,1},{1,0},{2,3},{3,2},{4,5},{5,4},{6,7},{7,6},{8,9},{9,8},{10,11... | collective-permute-start | bytes 5505032 | tf_op jit(solution)/shard_map/ppermute | solution.py:311
  165.0 5.1 %copy-start.8 = (bf16[256,512]{1,0:T(8,128)(2,1)S(1)}, bf16[256,512]{1,0:T(8,128)(2,1)}, u32[]{:S(2)}) copy-start(bf16[256,512]{1,0:T(8,128)(2,1)} %inward.3.refs_0_) | copy-start | bytes 786436
  165.0 43.9 %all-to-all-start.3 = ((bf16[16,8,3584]{2,1,0:T(8,128)(2,1)}), bf16[16,8,3584]{2,1,0:T(8,128)(2,1)S(1)}, u32[]{:S(2)}, u32[]{:S(2)}) async-start(bf16[16,8,3584]{2,1,0:T(8,128)(2,1)} %bitcast.39), calls=%async_computation.3 | async-start | bytes 1835008 | tf_op jit(solution)/shard_map/all_to_all | solution.py:315
  170.1 31.6 %collective-permute-start.1 = (bf16[256,512]{1,0:T(8,128)(2,1)S(1)}, bf16[256,512]{1,0:T(8,128)(2,1)S(1)}, u32[]{:S(2)}, u32[]{:S(2)}) collective-permute-start(bf16[256,512]{1,0:T(8,128)(2,1)S(1)} %copy-done.8), channel_id=1, source_target_pairs={{0,1},{1,0},{2,3},{3,2},{4,5},{5,4},{6,7},{7,6},{8,9},{9,8},{10,11... | collective-permute-start | bytes 786440 | tf_op jit(solution)/shard_map/ppermute | solution.py:311
  201.8 0.8 copy-start.12
  209.0 27.2 %copy-start.3 = (bf16[16,8,3584]{2,1,0:T(8,128)(2,1)}, bf16[16,8,3584]{2,1,0:T(8,128)(2,1)S(1)}, u32[]{:S(2)}) copy-start(bf16[16,8,3584]{2,1,0:T(8,128)(2,1)S(1)} %all-to-all-done.3) | copy-start | bytes 2752516
  209.0 45.3 %all-to-all-start.4 = ((bf16[32,8,3584]{2,1,0:T(8,128)(2,1)}), bf16[32,8,3584]{2,1,0:T(8,128)(2,1)S(1)}, u32[]{:S(2)}, u32[]{:S(2)}) async-start(bf16[32,8,3584]{2,1,0:T(8,128)(2,1)} %bitcast.33), calls=%async_computation.4 | async-start | bytes 3670016 | tf_op jit(solution)/shard_map/all_to_all | solution.py:328
  223.1 13.0 %collective-permute-start.3 = (bf16[256,512]{1,0:T(8,128)(2,1)}, bf16[256,512]{1,0:T(8,128)(2,1)S(1)}, u32[]{:S(2)}, u32[]{:S(2)}) collective-permute-start(bf16[256,512]{1,0:T(8,128)(2,1)} %inward.4.refs_0_), channel_id=1, source_target_pairs={{0,1},{1,0},{2,3},{3,2},{4,5},{5,4},{6,7},{7,6},{8,9},{9,8},{10,11... | collective-permute-start | bytes 786440 | tf_op jit(solution)/shard_map/ppermute | solution.py:311
  236.2 0.8 copy-start.11
  236.2 17.8 %collective-permute-start.4 = (bf16[64,3584]{1,0:T(8,128)(2,1)S(1)}, bf16[64,3584]{1,0:T(8,128)(2,1)S(1)}, u32[]{:S(2)}, u32[]{:S(2)}) collective-permute-start(bf16[64,3584]{1,0:T(8,128)(2,1)S(1)} %get-tuple-element.46), channel_id=1, source_target_pairs={{0,1},{1,0},{2,3},{3,2},{4,5},{5,4},{6,7},{7,6},{8,9},{9,8},{10,11... | collective-permute-start | bytes 1376264 | tf_op jit(solution)/shard_map/ppermute | solution.py:311
  254.1 0.8 copy-start.9
  254.3 1.2 copy-start.6
  255.5 57.5 %all-to-all-start.5 = ((bf16[32,8,3584]{2,1,0:T(8,128)(2,1)}), bf16[32,8,3584]{2,1,0:T(8,128)(2,1)}, u32[]{:S(2)}, u32[]{:S(2)}) async-start(bf16[32,8,3584]{2,1,0:T(8,128)(2,1)} %bitcast.32), calls=%async_computation.5 | async-start | bytes 3670016 | tf_op jit(solution)/shard_map/all_to_all | solution.py:328
  262.4 26.8 %collective-permute-start.5 = (bf16[64,3584]{1,0:T(8,128)(2,1)S(1)}, bf16[64,3584]{1,0:T(8,128)(2,1)S(1)}, u32[]{:S(2)}, u32[]{:S(2)}) collective-permute-start(bf16[64,3584]{1,0:T(8,128)(2,1)S(1)} %get-tuple-element.45), channel_id=1, source_target_pairs={{0,1},{1,0},{2,3},{3,2},{4,5},{5,4},{6,7},{7,6},{8,9},{9,8},{10,11... | collective-permute-start | bytes 1376264 | tf_op jit(solution)/shard_map/ppermute | solution.py:311
  289.2 0.8 copy-start.10
  298.7 6.2 %collective-permute-start.6 = (bf16[128,512]{1,0:T(8,128)(2,1)}, bf16[128,512]{1,0:T(8,128)(2,1)S(1)}, u32[]{:S(2)}, u32[]{:S(2)}) collective-permute-start(bf16[128,512]{1,0:T(8,128)(2,1)} %inward.5.refs_0_), channel_id=1, source_target_pairs={{0,1},{1,0},{2,3},{3,2},{4,5},{5,4},{6,7},{7,6},{8,9},{9,8},{10,11... | collective-permute-start | bytes 393224 | tf_op jit(solution)/shard_map/ppermute | solution.py:311
  304.9 0.7 copy-start.13
  313.0 29.6 %all-to-all-start.6 = ((bf16[32,8,1792]{2,1,0:T(8,128)(2,1)}), bf16[32,8,1792]{2,1,0:T(8,128)(2,1)S(1)}, u32[]{:S(2)}, u32[]{:S(2)}) async-start(bf16[32,8,1792]{2,1,0:T(8,128)(2,1)} %bitcast.35), calls=%async_computation.6 | async-start | bytes 1835008 | tf_op jit(solution)/shard_map/all_to_all | solution.py:328
  342.6 0.9 copy-start.7
  342.6 5.2 %copy-start.1 = (bf16[2048,448]{0,1:T(8,128)(2,1)S(1)}, bf16[2048,448]{0,1:T(8,128)(2,1)}, u32[]{:S(2)}) copy-start(bf16[2048,448]{0,1:T(8,128)(2,1)} %param.8) | copy-start | bytes 5505028
